TPU v7x, 32 devices: a whole 2x2x4 slice. The times are simulated.
32 devices in a mesh: space: 8 (over z, y), dp: 4 (over x, core).
Axes of the slice: x: 2, y: 2, z: 4, core: 2. Of those that a mesh axis runs over, the one named last changes fastest.
Arguments:
- features: bfloat16 [4, 4096, 128], P('dp', 'space'), may hold values from -6 to 6
- occupancy: int32 [4, 4096], P('dp', 'space'), may hold values from 0 to 1
- brick_pairs: int32 [4, 64, 27], P('dp', 'space'), may hold values from 0 to 24, as said below
- send_lists: int32 [4, 8, 16], P('dp', 'space'), may hold values from -1 to 7, as said below
- scan_weight: int32 [4], P('dp'), may hold values from 1 to 12
- kernel: bfloat16 [3456, 128], replicated, may hold values from -0.109375 to 0.109375
- cotangent: bfloat16 [4, 4096, 128], P('dp', 'space'), may hold values from -6 to 6
Outputs:
- output_features: bfloat16 [4, 4096, 128], P('dp', 'space')
- grad_features: bfloat16 [4, 4096, 128], P('dp', 'space')
- grad_kernel: float32 [3456, 128], replicated
Inputs may be any that keep to these rules, and one draw needn't show every extreme that they name: `brick_pairs`: entry 13 of brick b is b itself. A value under 8 is a brick of the same owner; 8 + t * 2 + k names entry k of what owner t sends to this owner, and then t differs from this owner's index on space in exactly one bit; 24 is an empty brick. `send_lists`: for a destination t that differs from the owner's index in exactly one bit, 2 distinct slots of the owner; for every other destination all -1.
All inputs are finite; a program needn't handle non-finite values.
Results may differ from a plain program's by a relative error of at most 0.0017.
Values may be sent and summed in bfloat16 or wider, within the bound.
A program may use at most 64 MiB of HBM per device.

v0:
```python
import math

import jax
import jax.numpy as jnp
import numpy as np
from jax import lax
from jax.sharding import PartitionSpec as P


def swapped(value, axis, bit):
    mask = 2**bit
    pairs = [(source, source ^ mask) for source in range(lax.axis_size(axis))]
    return lax.ppermute(value, axis, pairs)


def patch_layout():
    offset_list = []
    inner_list = []
    for pos_x in range(6):
        for pos_y in range(6):
            for pos_z in range(6):
                offset_parts = []
                inner_parts = []
                for coordinate in (pos_x, pos_y, pos_z):
                    shifted = coordinate - 1
                    brick_step = shifted // 4
                    offset_parts.append(brick_step + 1)
                    inner_parts.append(shifted - 4 * brick_step)
                offset_list.append(9 * offset_parts[0] + 3 * offset_parts[1] + offset_parts[2])
                inner_list.append(16 * inner_parts[0] + 4 * inner_parts[1] + inner_parts[2])
    return (np.array(offset_list, np.int32), np.array(inner_list, np.int32))


def convolve(table_rows, table_index, grad_in, kernel, offset_map, inner_map):
    bricks = table_index.shape[0]
    channels = table_rows.shape[1]
    patch_rows = table_index[:, offset_map] * 64 + inner_map[None, :]
    patch_cube = jnp.take(table_rows, patch_rows.reshape(-1), axis=0).reshape(
        bricks, 6, 6, 6, channels
    )
    result = jnp.zeros((bricks * 64, channels), jnp.float32)
    patch_grad = jnp.zeros((bricks, 6, 6, 6, channels), jnp.float32)
    weight_grads = []
    for shift_x in range(3):
        pieces = []
        for tap_index in range(9):
            shift_y = tap_index // 3
            shift_z = tap_index % 3
            pieces.append(
                patch_cube[
                    :, shift_x : shift_x + 4, shift_y : shift_y + 4, shift_z : shift_z + 4, :
                ].reshape(bricks * 64, channels)
            )
        columns = jnp.concatenate(pieces, axis=1)
        kernel_rows = kernel[shift_x * 9 * channels : (shift_x + 1) * 9 * channels]
        result = result + jnp.dot(columns, kernel_rows, preferred_element_type=jnp.float32)
        weight_grads.append(jnp.dot(columns.T, grad_in, preferred_element_type=jnp.float32))
        for tap_index in range(9):
            shift_y = tap_index // 3
            shift_z = tap_index % 3
            tap_weight = kernel_rows[tap_index * channels : (tap_index + 1) * channels]
            tap_grad = jnp.dot(grad_in, tap_weight.T, preferred_element_type=jnp.float32)
            patch_grad = patch_grad.at[
                :, shift_x : shift_x + 4, shift_y : shift_y + 4, shift_z : shift_z + 4, :
            ].add(tap_grad.reshape(bricks, 4, 4, 4, channels))
    table_grad = jax.ops.segment_sum(
        patch_grad.reshape(-1, channels), patch_rows.reshape(-1), num_segments=table_rows.shape[0]
    )
    return (result, table_grad, jnp.concatenate(weight_grads, axis=0))


def halo_index(pair_table, device, bricks, nspace, peer_cap, levels):
    zero_full = bricks + nspace * peer_cap
    relative = jnp.clip(pair_table - bricks, 0, nspace * peer_cap - 1)
    source = relative // peer_cap
    within = relative % peer_cap
    flipped = jnp.bitwise_xor(source, device)
    level_of = jnp.zeros_like(pair_table)
    for bit_level in range(levels):
        level_of = level_of + bit_level * (flipped == 1 << bit_level).astype(jnp.int32)
    compact = bricks + level_of * peer_cap + within
    outside = bricks + levels * peer_cap
    return jnp.where(
        pair_table < bricks, pair_table, jnp.where(pair_table >= zero_full, outside, compact)
    )


def pick_bricks(brick_rows, chosen):
    gathered = jnp.take(brick_rows, jnp.maximum(chosen, 0), axis=0)
    return jnp.where((chosen >= 0)[:, None], gathered, jnp.zeros_like(gathered))


def on_device(features, occupancy, brick_pairs, send_lists, scan_weight, kernel, cotangent):
    offset_list, inner_list = patch_layout()
    offset_map = jnp.asarray(offset_list, jnp.int32)
    inner_map = jnp.asarray(inner_list, jnp.int32)
    channels = features.shape[2]
    own_rows = features.shape[1]
    bricks = own_rows // 64
    nspace = lax.axis_size("space")
    scan_count = lax.axis_size("dp")
    levels = nspace.bit_length() - 1
    device = lax.axis_index("space")
    send_table = send_lists[0, 0]
    peer_cap = send_table.shape[0] // nspace
    voxel_mask = occupancy[0][:, None].astype(jnp.bfloat16)
    masked = features[0] * voxel_mask
    grad_in = cotangent[0] * voxel_mask
    brick_rows = masked.reshape(bricks, 64 * channels)
    empty_brick = jnp.zeros((1, 64 * channels), jnp.bfloat16)
    pair_table = brick_pairs[0]
    incoming = []
    for bit_level in range(levels):
        partner = jnp.bitwise_xor(device, 1 << bit_level)
        chosen = lax.dynamic_slice(send_table, (partner * peer_cap,), (peer_cap,))
        incoming.append(swapped(pick_bricks(brick_rows, chosen), "space", bit_level))
    brick_table = jnp.concatenate([brick_rows] + incoming + [empty_brick], axis=0).reshape(
        -1, channels
    )
    table_index = halo_index(pair_table, device, bricks, nspace, peer_cap, levels)
    result, table_grad, weight_grad = convolve(
        brick_table, table_index, grad_in, kernel, offset_map, inner_map
    )
    returned = jnp.zeros((bricks + 1, 64 * channels), jnp.float32)
    for bit_level in range(levels):
        partner = jnp.bitwise_xor(device, 1 << bit_level)
        chosen = lax.dynamic_slice(send_table, (partner * peer_cap,), (peer_cap,))
        start_row = own_rows + bit_level * peer_cap * 64
        grad_piece = (
            table_grad[start_row : start_row + peer_cap * 64]
            .astype(jnp.bfloat16)
            .reshape(peer_cap, 64 * channels)
        )
        came_back = swapped(grad_piece, "space", bit_level)
        target = jnp.where(chosen >= 0, chosen, bricks)
        returned = returned + jax.ops.segment_sum(
            came_back.astype(jnp.float32), target, num_segments=bricks + 1
        )
    returned = returned[:bricks]
    grad_sum = (
        grad_in.astype(jnp.float32) + table_grad[:own_rows] + returned.reshape(own_rows, channels)
    )
    own_weight = scan_weight[0].astype(jnp.float32)
    weighted = weight_grad * own_weight
    partial_sum, weight_total = lax.psum((weighted, own_weight), "dp")
    summed = lax.psum(partial_sum, "space")
    factor = own_weight * scan_count / weight_total
    mask_float = voxel_mask.astype(jnp.float32)
    output = (mask_float * (result + masked.astype(jnp.float32))).astype(jnp.bfloat16)
    grad_features = (factor * (mask_float * grad_sum)).astype(jnp.bfloat16)
    kernel_grad = summed * (scan_count / weight_total) / math.sqrt(64.0 * bricks * nspace)
    return (output[None], grad_features[None], kernel_grad)


def solution(mesh):
    return jax.shard_map(
        on_device,
        mesh=mesh,
        in_specs=(
            P("dp", "space", None),
            P("dp", "space"),
            P("dp", "space", None),
            P("dp", "space", None),
            P("dp"),
            P(),
            P("dp", "space", None),
        ),
        out_specs=(P("dp", "space", None), P("dp", "space", None), P()),
        check_vma=False,
    )
```

profile of v0, /device:TPU:1, one launch (start us, length us, event | category | flops | bytes accessed | tf_op | source)
XLA Modules:
  0.0 193.7 jit_solution(922437851422344203)
XLA Ops:
  7.3 0.9 compare_bitcast_fusion
  8.1 0.8 compare_and_fusion.1
  9.0 1.0 squeeze.16
  10.0 0.8 convert_reduce_fusion
  11.1 0.6 gather_fusion.2
  11.8 2.1 %collective-permute-start = (bf16[2,8192]{1,0:T(2,128)(2,1)S(1)}, bf16[2,8192]{1,0:T(2,128)(2,1)S(1)}, u32[]{:S(2)}, u32[]{:S(2)}) collective-permute-start(bf16[2,8192]{1,0:T(2,128)(2,1)S(1)} %broadcast_select_fusion.6), channel_id=1, source_target_pairs={{0,4},{4,0},{8,12},{12,8},{16,20},{20,16},{24,28},{28,24},{1,5},{5... | collective-permute-start | bytes 98312 | tf_op jit(solution)/shard_map/ppermute | solution.py:13
  13.9 0.6 gather_fusion.3
  14.6 1.4 collective-permute-start.1
  16.0 0.6 gather_fusion.4
  16.7 2.4 %collective-permute-start.2 = (bf16[2,8192]{1,0:T(2,128)(2,1)S(1)}, bf16[2,8192]{1,0:T(2,128)(2,1)S(1)}, u32[]{:S(2)}, u32[]{:S(2)}) collective-permute-start(bf16[2,8192]{1,0:T(2,128)(2,1)S(1)} %broadcast_select_fusion.4), channel_id=1, source_target_pairs={{0,16},{4,20},{8,24},{12,28},{16,0},{20,4},{24,8},{28,12},{1,17},{... | collective-permute-start | bytes 98312 | tf_op jit(solution)/shard_map/ppermute | solution.py:13
  19.3 0.7 gather_fusion
  21.0 0.2 fusion.25
  21.2 0.2 fusion.24
  21.4 0.2 fusion.23
  21.7 0.2 fusion.22
  21.9 0.6 fusion.119
  22.5 2.1 %fusion.21 = f32[8,6,6,6,128]{4,0,3,2,1:T(8,128)S(1)} fusion(f32[8,6,6,6,128]{4,0,3,2,1:T(8,128)S(1)} %fusion.22, s32[]{:T(128)} %bitcast.51, s32[]{:T(128)} %bitcast.52, s32[]{:T(128)} %bitcast.53, bf16[8,4,4,4,128]{4,0,3,2,1:T(8,128)(2,1)S(1)} %copy_multiply_fusion, bf16[3456,128]{1,0:T(8,128)(2,1)S(1)} %copy-done.1), kind=kOutput, calls=%fused_computation.52 | convolution fusion | flops 16842752 | bytes 688140 | tf_op jit(solution)/shard_map/dot_general | solution.py:62
  25.1 0.2 fusion.18
  25.3 0.2 fusion.17
  25.5 0.2 fusion.16
  25.8 0.2 fusion.15
  26.0 0.2 fusion.14
  26.2 0.2 fusion.13
  26.4 0.2 fusion.12
  27.1 0.2 fusion.9
  27.4 0.2 fusion.8
  27.6 0.2 fusion.7
  27.8 0.2 fusion.6
  29.1 0.2 reshape.1692
  29.3 3.9 %gather_fusion.1 = bf16[1728,128]{1,0:T(8,128)(2,1)S(1)} fusion(bf16[960,128]{1,0:T(8,128)(2,1)S(1)} %reshape.1692, s32[2048]{0:T(1024)S(1)} %pad_clamp_fusion), kind=kCustom, calls=%fused_computation.4 | custom fusion | bytes 891648 | tf_op jit(solution)/shard_map/jit(_take)/gather | solution.py:38
  33.4 0.5 broadcast_select_fusion
  33.9 0.5 fusion.117
  34.4 1.4 fusion.116
  36.3 0.6 fusion.49
  37.0 0.3 copy-done.3
  37.5 0.6 fusion.50
  38.5 0.6 fusion.51
  39.1 1.3 maximum_multiply_fusion
  40.4 0.2 all-reduce.6.cloned.1.call-start
  40.7 1.0 fusion.5
  41.6 1.0 fusion.4
  42.6 1.0 fusion.3
  43.6 1.0 fusion.2
  44.6 40.1 %all-reduce.4.cloned.1.call-done = f32[3456,128]{1,0:T(8,128)} async-done(((f32[3456,128]{1,0:T(8,128)}), f32[3456,128]{1,0:T(8,128)}) %all-reduce.4.cloned.1.call-update) | async-done | bytes 1769488 | tf_op jit(solution)/shard_map/psum | solution.py:145
  84.7 1.0 fusion.1
  85.8 1.0 fusion
  86.8 1.2 copy.31
  88.0 2.3 %reshape.1772 = f32[1728,128]{1,0:T(8,128)} reshape(f32[8,6,6,6,128]{4,3,2,1,0:T(8,128)} %copy.31) | data formatting | bytes 1769472 | tf_op jit(solution)/shard_map/reshape | solution.py:67
  90.3 12.0 %scatter_custom_fusion = f32[960,128]{1,0:T(8,128)S(1)} fusion(s32[1728]{0:T(1024)S(1)} %reshape.1770, f32[1728,128]{1,0:T(8,128)} %reshape.1772, f32[]{:T(128)} %constant.975.clone.1), kind=kCustom, calls=%fused_computation.81 | custom fusion | flops 221184 | bytes 492032 | tf_op jit(solution)/shard_map/scatter-add | solution.py:66
  102.4 2.2 %collective-permute-start.5 = (bf16[2,8192]{1,0:T(2,128)(2,1)S(1)}, bf16[2,8192]{1,0:T(2,128)(2,1)S(1)}, u32[]{:S(2)}, u32[]{:S(2)}) collective-permute-start(bf16[2,8192]{1,0:T(2,128)(2,1)S(1)} %reshape.1726), channel_id=1, source_target_pairs={{0,16},{4,20},{8,24},{12,28},{16,0},{20,4},{24,8},{28,12},{1,17},{... | collective-permute-start | bytes 98312 | tf_op jit(solution)/shard_map/ppermute | solution.py:13
  104.6 1.3 collective-permute-start.4
  105.9 1.3 collective-permute-start.3
  107.3 7.8 %psum.21 = f32[]{:T(128)} all-reduce(f32[]{:T(128)} %bitcast.38), channel_id=1, replica_groups=mesh['space'=8,'dp'=4] {'dp'}, use_global_device_ids=true, to_apply=%region_0.0 | all-reduce | flops 1 | bytes 8 | tf_op jit(solution)/shard_map/psum | solution.py:145
  116.5 0.6 copy-done.8
  117.1 1.3 scatter_custom_fusion.1
  118.4 0.7 slice.1593
  119.1 1.7 reshape.1727
  120.8 1.5 fusion.32
  122.4 0.5 convolution_add_fusion.27
  122.9 0.8 copy-done.4
  123.7 1.1 fusion.29
  124.8 0.9 fusion.43
  125.7 58.4 %all-reduce.6.cloned.1.call-done = f32[3456,128]{1,0:T(8,128)} async-done(((f32[3456,128]{1,0:T(8,128)}), f32[3456,128]{1,0:T(8,128)}) %all-reduce.6.cloned.1.call-update) | async-done | bytes 1769488 | tf_op jit(solution)/shard_map/psum | solution.py:146
  184.0 2.8 %multiply_multiply_fusion = f32[3456,128]{1,0:T(8,128)} fusion(f32[3456,128]{1,0:T(8,128)} %all-reduce.6.cloned.1.call-done, f32[]{:T(128)S(6)} %div.26), kind=kLoop, calls=%fused_computation.8 | loop fusion | flops 884736 | bytes 3538948 | tf_op jit(solution)/shard_map/div | solution.py:151
  (101 shorter events, 4.5 us)
Async XLA Ops:
  7.2 12.2 %copy-start.12 = (s32[216]{0:T(256)S(1)}, s32[216]{0:T(256)}, u32[]{:S(2)}) copy-start(s32[216]{0:T(256)} %constant.992) | copy-start | bytes 2596
  7.2 12.9 %copy-start.11 = (s32[216]{0:T(256)S(1)}, s32[216]{0:T(256)}, u32[]{:S(2)}) copy-start(s32[216]{0:T(256)} %constant.978.clone) | copy-start | bytes 2596
  7.2 12.0 %copy-start.10 = (s32[1,8,27]{2,1,0:T(8,128)S(1)}, s32[1,8,27]{2,1,0:T(8,128)}, u32[]{:S(2)}) copy-start(s32[1,8,27]{2,1,0:T(8,128)} %param.67) | copy-start | bytes 2596
  7.2 13.4 %copy-start = (bf16[1,512,128]{2,1,0:T(8,128)(2,1)S(1)}, bf16[1,512,128]{2,1,0:T(8,128)(2,1)}, u32[]{:S(2)}) copy-start(bf16[1,512,128]{2,1,0:T(8,128)(2,1)} %param.71) | copy-start | bytes 393220
  7.2 77.5 %all-reduce.4.cloned.1.call-start = ((), (), s32[]{:S(2)}) async-start(), calls=%async_computation | async-start | bytes 3538944 | tf_op jit(solution)/shard_map/psum | solution.py:145
  9.9 10.8 %copy-start.1 = (bf16[3456,128]{1,0:T(8,128)(2,1)S(1)}, bf16[3456,128]{1,0:T(8,128)(2,1)}, u32[]{:S(2)}) copy-start(bf16[3456,128]{1,0:T(8,128)(2,1)} %param.70) | copy-start | bytes 2654212
  11.8 17.0 %collective-permute-start = (bf16[2,8192]{1,0:T(2,128)(2,1)S(1)}, bf16[2,8192]{1,0:T(2,128)(2,1)S(1)}, u32[]{:S(2)}, u32[]{:S(2)}) collective-permute-start(bf16[2,8192]{1,0:T(2,128)(2,1)S(1)} %broadcast_select_fusion.6), channel_id=1, source_target_pairs={{0,4},{4,0},{8,12},{12,8},{16,20},{20,16},{24,28},{28,24},{1,5},{5... | collective-permute-start | bytes 98312 | tf_op jit(solution)/shard_map/ppermute | solution.py:13
  14.6 14.2 %collective-permute-start.1 = (bf16[2,8192]{1,0:T(2,128)(2,1)S(1)}, bf16[2,8192]{1,0:T(2,128)(2,1)S(1)}, u32[]{:S(2)}, u32[]{:S(2)}) collective-permute-start(bf16[2,8192]{1,0:T(2,128)(2,1)S(1)} %broadcast_select_fusion.5), channel_id=1, source_target_pairs={{0,8},{4,12},{8,0},{12,4},{16,24},{20,28},{24,16},{28,20},{1,9},{5... | collective-permute-start | bytes 98312 | tf_op jit(solution)/shard_map/ppermute | solution.py:13
  16.7 12.2 %collective-permute-start.2 = (bf16[2,8192]{1,0:T(2,128)(2,1)S(1)}, bf16[2,8192]{1,0:T(2,128)(2,1)S(1)}, u32[]{:S(2)}, u32[]{:S(2)}) collective-permute-start(bf16[2,8192]{1,0:T(2,128)(2,1)S(1)} %broadcast_select_fusion.4), channel_id=1, source_target_pairs={{0,16},{4,20},{8,24},{12,28},{16,0},{20,4},{24,8},{28,12},{1,17},{... | collective-permute-start | bytes 98312 | tf_op jit(solution)/shard_map/ppermute | solution.py:13
  27.3 0.7 copy-start.9
  36.3 1.0 copy-start.3
  40.4 143.6 %all-reduce.6.cloned.1.call-start = ((), (), s32[]{:S(2)}) async-start(), calls=%async_computation.1 | async-start | bytes 3538944 | tf_op jit(solution)/shard_map/psum | solution.py:146
  90.3 16.8 %copy-start.7 = (s32[1,1,16]{2,1,0:T(1,128)S(1)}, s32[1,1,16]{2,1,0:T(1,128)}, u32[]{:S(2)}) copy-start(s32[1,1,16]{2,1,0:T(1,128)} %param.68) | copy-start | bytes 196
  102.4 14.1 %collective-permute-start.5 = (bf16[2,8192]{1,0:T(2,128)(2,1)S(1)}, bf16[2,8192]{1,0:T(2,128)(2,1)S(1)}, u32[]{:S(2)}, u32[]{:S(2)}) collective-permute-start(bf16[2,8192]{1,0:T(2,128)(2,1)S(1)} %reshape.1726), channel_id=1, source_target_pairs={{0,16},{4,20},{8,24},{12,28},{16,0},{20,4},{24,8},{28,12},{1,17},{... | collective-permute-start | bytes 98312 | tf_op jit(solution)/shard_map/ppermute | solution.py:13
  104.6 11.9 %collective-permute-start.4 = (bf16[2,8192]{1,0:T(2,128)(2,1)S(1)}, bf16[2,8192]{1,0:T(2,128)(2,1)S(1)}, u32[]{:S(2)}, u32[]{:S(2)}) collective-permute-start(bf16[2,8192]{1,0:T(2,128)(2,1)S(1)} %reshape.1725), channel_id=1, source_target_pairs={{0,8},{4,12},{8,0},{12,4},{16,24},{20,28},{24,16},{28,20},{1,9},{5... | collective-permute-start | bytes 98312 | tf_op jit(solution)/shard_map/ppermute | solution.py:13
  105.9 11.2 %collective-permute-start.3 = (bf16[2,8192]{1,0:T(2,128)(2,1)S(1)}, bf16[2,8192]{1,0:T(2,128)(2,1)}, u32[]{:S(2)}, u32[]{:S(2)}) collective-permute-start(bf16[2,8192]{1,0:T(2,128)(2,1)S(1)} %reshape.1724), channel_id=1, source_target_pairs={{0,4},{4,0},{8,12},{12,8},{16,20},{20,16},{24,28},{28,24},{1,5},{5... | collective-permute-start | bytes 98312 | tf_op jit(solution)/shard_map/ppermute | solution.py:13
  116.5 0.6 copy-start.8
  120.8 1.5 copy-start.2
  122.4 1.3 copy-start.4
  122.4 1.3 copy-start.6
  123.7 1.1 copy-start.5
Sparse Core Ops, SparseCore 0:
  40.5 44.0 all-reduce.3
  88.7 95.2 all-reduce.5
where the time goes:
time: 195 us; the launch traced here: 194 us
  waiting for transfers between devices  98.5 us (51%)
  other arithmetic  22.2 us (11%)
  local copies, waits for them, and re-layouts  20.3 us (10%)
  matrix products  17.2 us (9%)
  between operations  16.9 us (9%)
  starting transfers between devices  10.9 us (6%)
  blocking collectives  7.79 us (4%)
    psum x1, waiting for transfers between devices, on_device(): summed = lax.psum(partial_sum, 'space')  58.4 us
    psum x1, waiting for transfers between devices, on_device(): partial_sum, weight_total = lax.psum((weighted, own_weight), 'dp')  40.1 us
    dot_general x27, matrix products, convolve(): jnp.dot(grad_in, tap_weight.T, preferred_element_type=jnp.float32)  12.3 us
    scatter-add x1, other arithmetic, convolve(): jax.ops.segment_sum(patch_grad.reshape(-1, channels), patch_rows.reshape(...  12 us
    ppermute x6, starting transfers between devices, swapped(): return lax.ppermute(value, axis, pairs)  10.6 us
    psum x1, blocking collectives, on_device(): partial_sum, weight_total = lax.psum((weighted, own_weight), 'dp')  7.79 us
    gather x2, local copies, waits for them, and re-layouts, convolve(): jnp.take(table_rows, patch_rows.reshape(-1), axis=0)  4.06 us
  transfers between devices with their start and end apart: 8, of which 2 were waited for; matrix products, arithmetic and copies ran while one was open for 20% of the time, Pallas kernels for 0%

commit v1 on v0

v1 whole, which is shorter than its diff:
```python
import functools
import math

import jax
import jax.numpy as jnp
import numpy as np
from jax import lax
from jax.experimental import pallas as pl
from jax.experimental.pallas import tpu as pltpu
from jax.sharding import PartitionSpec as P

MESH = pl.DeviceIdType.MESH
VOXELS = 64
TAPS = 27


def axis_places(step):
    return {-1: [(0, 3)], 0: [(1, 0), (2, 1), (3, 2), (4, 3)], 1: [(5, 0)]}[step]


def slab(offset):
    steps = (offset // 9 - 1, offset // 3 % 3 - 1, offset % 3 - 1)
    places = []
    for px, vx in axis_places(steps[0]):
        for py, vy in axis_places(steps[1]):
            for pz, vz in axis_places(steps[2]):
                places.append(((px, py, pz), 16 * vx + 4 * vy + vz))
    return places


def voxel_classes():
    readers = {}
    for offset in range(TAPS):
        for pos, voxel in slab(offset):
            readers.setdefault(voxel, []).append((offset, pos))
    classes = {}
    for voxel in range(VOXELS):
        key = tuple(o for o, _ in readers[voxel])
        classes.setdefault(key, []).append((voxel, [pos for _, pos in readers[voxel]]))
    return classes


def kernel_body(sizes, scale, feat, occ, pairs_s, pairs_v, sends, weight, ker, cot,
                out_f, out_g, out_k,
                mask, fnat, table, gnat, gvox, patch, pgrad, cols, tgrad, conv, wgrad,
                halo_out, halo_in, back_out, back_in, wsend, wrecv,
                core_in, half_in, tail_in, tail_sum, send_sem, recv_sem):
    nspace, ndp, cap, bricks, chan = sizes
    ls, ld = nspace.bit_length() - 1, ndp.bit_length() - 1
    own = bricks * VOXELS
    index = {"space": lax.axis_index("space"), "dp": lax.axis_index("dp")}

    def bit_of(bit):
        axis, level = bit
        return lax.rem(index[axis] // (1 << level), 2)

    def peer_index(bit):
        return index[bit[0]] + (1 - 2 * bit_of(bit)) * (1 << bit[1])

    all_bits = [("dp", i) for i in range(ld)] + [("space", i) for i in range(ls)]
    barrier = pltpu.get_barrier_semaphore()
    for bit in all_bits:
        pl.semaphore_signal(barrier, inc=1, device_id={bit[0]: peer_index(bit)},
                            device_id_type=MESH)

    started = []

    def send(src, dst, bit):
        n = len(started)
        copy = pltpu.make_async_remote_copy(
            src_ref=src, dst_ref=dst, send_sem=send_sem.at[n], recv_sem=recv_sem.at[n],
            device_id={bit[0]: peer_index(bit)}, device_id_type=MESH)
        copy.start()
        started.append(copy)
        return copy

    for i in range(own // 128):
        row = occ[0:1, i * 128:(i + 1) * 128].astype(jnp.float32)
        mask[i * 128:(i + 1) * 128, :] = jnp.transpose(jnp.broadcast_to(row, (128, 128)))
    fnat[...] = feat[0].astype(jnp.float32) * mask[...]
    table[0:bricks] = fnat[...].reshape(bricks, VOXELS, chan)
    table[bricks + nspace * cap] = jnp.zeros((VOXELS, chan), jnp.float32)

    picks = []
    for level in range(ls):
        partner = peer_index(("space", level))
        for k in range(cap):
            chosen = sends[0, 0, partner * cap + k]
            picks.append(chosen)
            live = jnp.full((VOXELS, chan), chosen, jnp.int32) >= 0
            at = (level * cap + k) * VOXELS
            brick = table[jnp.maximum(chosen, 0)]
            halo_out[at:at + VOXELS, :] = jnp.where(live, brick, 0.0).astype(jnp.bfloat16)
    own_weight = weight[0].astype(jnp.float32)
    wsend[0] = jnp.full((8, 128), own_weight, jnp.float32)

    pl.semaphore_wait(barrier, len(all_bits))
    rows = cap * VOXELS
    halo = [send(halo_out.at[pl.ds(level * rows, rows)], halo_in.at[pl.ds(level * rows, rows)],
                 ("space", level)) for level in range(ls)]
    wcopy = send(wsend.at[0], wrecv.at[0], ("dp", 0))

    gnat[...] = cot[0].astype(jnp.float32) * mask[...]
    for v in range(VOXELS):
        gvox[v * 8:(v + 1) * 8, :] = gnat[pl.ds(v, bricks, stride=VOXELS), :]
    grad = gvox[...].astype(jnp.bfloat16)
    for pos, v in slab(13):
        patch[pos[0], pos[1], pos[2]] = fnat[pl.ds(v, bricks, stride=VOXELS), :]
    pgrad[...] = jnp.zeros(pgrad.shape, jnp.float32)

    def spread(taps):
        for tap in taps:
            a, b, c = tap // 9, tap // 3 % 3, tap % 3
            part = lax.dot_general(grad, ker[tap * chan:(tap + 1) * chan, :],
                                   (((1,), (1,)), ((), ())), preferred_element_type=jnp.float32)
            pgrad[a:a + 4, b:b + 4, c:c + 4] += part.reshape(4, 4, 4, bricks, chan)

    spread(range(0, 9))

    for level in range(ls):
        halo[level].wait_recv()
        entry = bricks + peer_index(("space", level)) * cap
        for k in range(cap):
            at = level * rows + k * VOXELS
            table[entry + k] = halo_in[at:at + VOXELS, :].astype(jnp.float32)
    for level in range(ld):
        wcopy.wait_recv()
        wsend[level + 1] = wsend[level] + wrecv[level]
        if level + 1 < ld:
            wcopy = send(wsend.at[level + 1], wrecv.at[level + 1], ("dp", level + 1))
    for b in range(bricks):
        for offset in range(TAPS):
            if offset != 13:
                entry = pairs_s[0, b, offset]
                for pos, v in slab(offset):
                    patch[pos[0], pos[1], pos[2], b:b + 1, :] = table[entry, v:v + 1, :]

    for tap in range(TAPS):
        a, b, c = tap // 9, tap // 3 % 3, tap % 3
        cols[:, tap * chan:(tap + 1) * chan] = patch[a:a + 4, b:b + 4, c:c + 4].reshape(
            own, chan).astype(jnp.bfloat16)

    total_rows = TAPS * chan
    half_rows = total_rows // 2
    part_rows = half_rows // 3
    first, rest = all_bits[0], all_bits[1:]
    turn, tail = rest[:3], rest[3:]
    orders = [[turn[(p + j) % 3] for j in range(3)] for p in range(3)]
    mine = bit_of(first)

    def weigh(taps):
        lo, hi = taps[0] * chan, (taps[-1] + 1) * chan
        wgrad[lo:hi, :] = own_weight * lax.dot_general(
            cols[:, lo:hi], grad, (((0,), (0,)), ((), ())), preferred_element_type=jnp.float32)

    def tile8(x):
        return pl.multiple_of(x, 8)

    cores = []
    done = 0
    for p in range(3):
        low_end = -(-(p + 1) * part_rows // chan)
        mid = half_rows // chan
        high_end = -(-(half_rows + (p + 1) * part_rows) // chan)
        low_end = min(low_end, mid)
        if p == 0:
            low_at, high_at = 0, mid
        if low_end > low_at:
            weigh(list(range(low_at, low_end)))
        weigh(list(range(high_at, high_end)))
        low_at, high_at = low_end, high_end
        src = tile8((1 - mine) * half_rows + p * part_rows)
        cores.append(send(wgrad.at[pl.ds(src, part_rows)], core_in.at[p], first))

    offs = [mine * half_rows + p * part_rows for p in range(3)]
    flight = list(cores)
    width = part_rows

    def reduce_stage(j):
        for p in range(3):
            flight[p].wait_recv()
            size = part_rows >> min(j, 3)
            off = tile8(offs[p])
            if j == 0:
                wgrad[pl.ds(off, size), :] += core_in[p]
            elif j <= 3:
                at = part_rows - (part_rows >> (j - 1))
                wgrad[pl.ds(off, size), :] += half_in[p, at:at + size, :]
            else:
                i = j - 4
                held = wgrad[pl.ds(off, size), :] if i == 0 else tail_sum[p, i - 1]
                tail_sum[p, i] = held + tail_in[p, i]
            if j < 3:
                bit = orders[p][j]
                half = size // 2
                at = part_rows - (part_rows >> j)
                other = tile8(offs[p] + (1 - bit_of(bit)) * half)
                flight[p] = send(wgrad.at[pl.ds(other, half)],
                                 half_in.at[p, pl.ds(at, half)], bit)
                offs[p] = offs[p] + bit_of(bit) * half
            elif j - 3 < len(tail):
                i = j - 3
                src = wgrad.at[pl.ds(off, size)] if i == 0 else tail_sum.at[p, i - 1]
                flight[p] = send(src, tail_in.at[p, i], tail[i])

    reduce_stage(0)
    spread(range(9, 18))
    reduce_stage(1)
    spread(range(18, 27))

    entries = tgrad.shape[0] // VOXELS
    lane = lax.broadcasted_iota(jnp.int32, (1, 128), 1)
    code = jnp.where(lane < bricks, lane, -1)
    for level in range(ls):
        for k in range(cap):
            name = bricks + peer_index(("space", level)) * cap + k
            code = jnp.where(lane == bricks + level * cap + k, name, code)
    hits = {}
    for offset in range(TAPS):
        hit = pairs_v[0, :, offset:offset + 1] == code
        hits[offset] = jnp.where(hit, 1.0, 0.0).astype(jnp.float32)
    for offsets, voxels in voxel_classes().items():
        left = jnp.concatenate([hits[o] for o in offsets] * 2, axis=0).astype(jnp.bfloat16)
        right = jnp.concatenate(
            [jnp.concatenate([pgrad[pos[j][0], pos[j][1], pos[j][2]] for _, pos in voxels], axis=1)
             for j in range(len(offsets))], axis=0)
        high = right.astype(jnp.bfloat16)
        low = (right - high.astype(jnp.float32)).astype(jnp.bfloat16)
        sums = lax.dot_general(left, jnp.concatenate([high, low], axis=0),
                               (((0,), (0,)), ((), ())), preferred_element_type=jnp.float32)
        for n, (v, _) in enumerate(voxels):
            for t in range(0, entries, 8):
                tgrad[pl.ds(t * VOXELS + v, 8, stride=VOXELS), :] = sums[t:t + 8,
                                                                        n * chan:(n + 1) * chan]
    back_out[...] = tgrad[own:own + ls * rows, :].astype(jnp.bfloat16)
    back = [send(back_out.at[pl.ds(level * rows, rows)], back_in.at[pl.ds(level * rows, rows)],
                 ("space", level)) for level in range(ls)]

    reduce_stage(2)
    third = TAPS // 3 * chan

    def convolve(i):
        return jnp.dot(cols[:, i * third:(i + 1) * third], ker[i * third:(i + 1) * third, :],
                       preferred_element_type=jnp.float32)

    conv[...] = convolve(0) + patch[1:5, 1:5, 1:5].reshape(own, chan)
    reduce_stage(3)
    conv[...] += convolve(1)
    for j in range(len(tail)):
        reduce_stage(4 + j)
    total = wsend[ld][0:1, :]
    last = part_rows >> 3
    kernel_scale = (ndp / total) * scale
    for p in range(3):
        off = tile8(offs[p])
        held = tail_sum[p, len(tail) - 1] if tail else wgrad[pl.ds(off, last), :]
        out_k[pl.ds(off, last), :] = held * kernel_scale

    def gather_start(j):
        for p in range(3):
            size = part_rows >> j
            off = tile8(offs[p])
            bit = orders[p][j - 1] if j else first
            flight[p] = send(out_k.at[pl.ds(off, size)], out_k.at[pl.ds(off, size)], bit)
            if j:
                offs[p] = offs[p] - bit_of(bit) * size

    def gather_wait():
        for p in range(3):
            flight[p].wait_recv()

    gather_start(3)
    conv[...] += convolve(2)
    gather_wait()
    gather_start(2)
    for v in range(VOXELS):
        gvox[pl.ds(v, bricks, stride=VOXELS), :] = conv[v * 8:(v + 1) * 8, :]
    out_f[0] = (gvox[...] * mask[...]).astype(jnp.bfloat16)
    gather_wait()
    gather_start(1)
    for copy in back:
        copy.wait_recv()
    factor = own_weight * ndp / total
    for b in range(bricks):
        lo, hi = b * VOXELS, (b + 1) * VOXELS
        held = gnat[lo:hi, :] + tgrad[lo:hi, :]
        for e, chosen in enumerate(picks):
            came = back_in[e * VOXELS:(e + 1) * VOXELS, :].astype(jnp.float32)
            here = jnp.full((VOXELS, chan), chosen, jnp.int32) == b
            held = held + jnp.where(here, came, 0.0)
        out_g[0, lo:hi, :] = (factor * (mask[lo:hi, :] * held)).astype(jnp.bfloat16)
    gather_wait()
    gather_start(0)
    gather_wait()
    for copy in started:
        copy.wait_send()


def on_device(features, occupancy, brick_pairs, send_lists, scan_weight, kernel, cotangent):
    nspace, ndp = lax.axis_size("space"), lax.axis_size("dp")
    own, chan = features.shape[1:]
    bricks = own // VOXELS
    cap = send_lists.shape[2] // nspace
    ls, ld = nspace.bit_length() - 1, ndp.bit_length() - 1
    entries = -(-(bricks + ls * cap) // 8) * 8
    rows = TAPS * chan
    part = rows // 6
    tail = max(ls + ld - 4, 1)
    copies = 2 * ls + ld + 3 * (1 + 3 + (ls + ld - 4) + 4)
    f32, bf16 = jnp.float32, jnp.bfloat16
    vmem, smem = pl.BlockSpec(memory_space=pltpu.VMEM), pl.BlockSpec(memory_space=pltpu.SMEM)
    scale = 1.0 / math.sqrt(64.0 * bricks * nspace)
    return pl.pallas_call(
        functools.partial(kernel_body, (nspace, ndp, cap, bricks, chan), scale),
        out_shape=(
            jax.ShapeDtypeStruct(features.shape, bf16),
            jax.ShapeDtypeStruct(features.shape, bf16),
            jax.ShapeDtypeStruct((rows, chan), f32),
        ),
        in_specs=[vmem, vmem, smem, vmem, smem, smem, vmem, vmem],
        out_specs=(vmem, vmem, vmem),
        scratch_shapes=[
            pltpu.VMEM((own, chan), f32),
            pltpu.VMEM((own, chan), f32),
            pltpu.VMEM((bricks + nspace * cap + 1, VOXELS, chan), f32),
            pltpu.VMEM((own, chan), f32),
            pltpu.VMEM((own, chan), f32),
            pltpu.VMEM((6, 6, 6, bricks, chan), f32),
            pltpu.VMEM((6, 6, 6, bricks, chan), f32),
            pltpu.VMEM((own, rows), bf16),
            pltpu.VMEM((entries * VOXELS, chan), f32),
            pltpu.VMEM((own, chan), f32),
            pltpu.VMEM((rows, chan), f32),
            pltpu.VMEM((ls * cap * VOXELS, chan), bf16),
            pltpu.VMEM((ls * cap * VOXELS, chan), bf16),
            pltpu.VMEM((ls * cap * VOXELS, chan), bf16),
            pltpu.VMEM((ls * cap * VOXELS, chan), bf16),
            pltpu.VMEM((ld + 1, 8, 128), f32),
            pltpu.VMEM((ld, 8, 128), f32),
            pltpu.VMEM((3, part, chan), f32),
            pltpu.VMEM((3, part, chan), f32),
            pltpu.VMEM((3, tail, part // 8, chan), f32),
            pltpu.VMEM((3, tail, part // 8, chan), f32),
            pltpu.SemaphoreType.DMA((copies,)),
            pltpu.SemaphoreType.DMA((copies,)),
        ],
        compiler_params=pltpu.CompilerParams(
            collective_id=0, has_side_effects=True, vmem_limit_bytes=50 * 1024 * 1024
        ),
        cost_estimate=pl.CostEstimate(flops=6 * own * rows * chan, bytes_accessed=6 * 2**20,
                                      transcendentals=0),
    )(features, occupancy, brick_pairs, brick_pairs, send_lists, scan_weight, kernel, cotangent)


def solution(mesh):
    return jax.shard_map(
        on_device,
        mesh=mesh,
        in_specs=(
            P("dp", "space", None),
            P("dp", "space"),
            P("dp", "space", None),
            P("dp", "space", None),
            P("dp"),
            P(),
            P("dp", "space", None),
        ),
        out_specs=(P("dp", "space", None), P("dp", "space", None), P()),
        check_vma=False,
    )
```

time: 195 us -> 54.8 us (0.28)
  waiting for transfers between devices: 98.5 us -> 0 us
  Pallas kernels: 0 us -> 45.7 us
  other arithmetic: 22.2 us -> 0 us
  matrix products: 17.2 us -> 0 us
  between operations: 16.9 us -> 1.3 us
  local copies, waits for them, and re-layouts: 20.3 us -> 7.51 us
  starting transfers between devices: 10.9 us -> 0 us
  blocking collectives: 7.79 us -> 0 us
    psum x2 -> x0, waiting for transfers between devices: 98.4 us -> none  [the longest x1 58.4 us: on_device(): summed = lax.psum(partial_sum, 'space')]
    pallas_call x0 -> x1, Pallas kernels: none -> 45.7 us  [on_device(): pl.pallas_call(functools.partial(kernel_body, (nspace, ndp, cap, bricks,...]
    dot_general x33 -> x0, matrix products: 17.2 us -> none  [the longest x27 12.3 us: convolve(): jnp.dot(grad_in, tap_weight.T, preferred_element_type=jnp.float32)]
    scatter-add x1 -> x0, other arithmetic: 12 us -> none  [convolve(): jax.ops.segment_sum(patch_grad.reshape(-1, channels), patch_rows.reshape(...]
    ppermute x6 -> x0, starting transfers between devices: 10.6 us -> none  [swapped(): return lax.ppermute(value, axis, pairs)]
    psum x1 -> x0, blocking collectives: 7.79 us -> none  [on_device(): partial_sum, weight_total = lax.psum((weighted, own_weight), 'dp')]
    gather x7 -> x0, local copies, waits for them, and re-layouts: 6.6 us -> none  [the longest x2 4.06 us: convolve(): jnp.take(table_rows, patch_rows.reshape(-1), axis=0)]
    unnamed x51 -> x15, local copies, waits for them, and re-layouts: 2.73 us -> 7.51 us
  transfers between devices with their start and end apart: 8 -> 0, of which waited for: 2 -> 0; matrix products, arithmetic and copies ran while one was open for 20% -> 0% of each run, Pallas kernels for 0% -> 0%
where the time goes in v1:
time: 54.8 us; the launch traced here: 54.5 us
  Pallas kernels  45.7 us (83%)
  local copies, waits for them, and re-layouts  7.51 us (14%)
  between operations  1.3 us (2%)
    pallas_call x1, Pallas kernels, on_device(): pl.pallas_call(functools.partial(kernel_body, (nspace, ndp, cap, bricks,...  45.7 us
    unnamed x15, local copies, waits for them, and re-layouts  7.51 us

profile of v1, /device:TPU:1, one launch (start us, length us, event | category | flops | bytes accessed | tf_op | source)
XLA Modules:
  0.0 54.5 jit_solution(9860874525268310072)
XLA Ops:
  1.3 0.0 copy-start
  1.3 1.2 %copy-done = bf16[3456,128]{1,0:T(8,128)(2,1)S(1)} copy-done((bf16[3456,128]{1,0:T(8,128)(2,1)S(1)}, bf16[3456,128]{1,0:T(8,128)(2,1)}, u32[]{:S(2)}) %copy-start) | copy-done | bytes 884760
  2.4 0.0 copy-start.1
  2.4 0.9 %copy-done.1 = bf16[1,512,128]{2,1,0:T(8,128)(2,1)S(1)} copy-done((bf16[1,512,128]{2,1,0:T(8,128)(2,1)S(1)}, bf16[1,512,128]{2,1,0:T(8,128)(2,1)}, u32[]{:S(2)}) %copy-start.1) | copy-done | bytes 131096
  3.4 0.0 copy-start.2
  3.4 0.9 %copy-done.2 = bf16[1,512,128]{2,1,0:T(8,128)(2,1)S(1)} copy-done((bf16[1,512,128]{2,1,0:T(8,128)(2,1)S(1)}, bf16[1,512,128]{2,1,0:T(8,128)(2,1)}, u32[]{:S(2)}) %copy-start.2) | copy-done | bytes 131096
  4.3 0.0 copy-start.3
  4.3 0.7 %copy-done.3 = s32[1,8,27]{2,1,0:T(8,128)S(1)} copy-done((s32[1,8,27]{2,1,0:T(8,128)S(1)}, s32[1,8,27]{2,1,0:T(8,128)}, u32[]{:S(2)}) %copy-start.3) | copy-done | bytes 888
  4.9 0.0 copy-start.4
  4.9 0.7 %copy-done.4 = s32[1,512]{1,0:T(1,128)S(1)} copy-done((s32[1,512]{1,0:T(1,128)S(1)}, s32[1,512]{1,0:T(1,128)}, u32[]{:S(2)}) %copy-start.4) | copy-done | bytes 2072
  5.6 0.0 copy-start.5
  5.6 0.7 %copy-done.5 = s32[1,1,16]{2,1,0:T(1,128)S(1)} copy-done((s32[1,1,16]{2,1,0:T(1,128)S(1)}, s32[1,1,16]{2,1,0:T(1,128)}, u32[]{:S(2)}) %copy-start.5) | copy-done | bytes 88
  6.3 45.7 %shard_map.94 = (bf16[1,512,128]{2,1,0:T(8,128)(2,1)S(1)}, bf16[1,512,128]{2,1,0:T(8,128)(2,1)S(1)}, f32[3456,128]{1,0:T(8,128)S(1)}) custom-call(bf16[1,512,128]{2,1,0:T(8,128)(2,1)S(1)} %copy-done.1, s32[1,512]{1,0:T(1,128)S(1)} %copy-done.4, s32[1,8,27]{2,1,0:T(8,128)S(1)} %copy-done.3, s32[1,8,27]{2,1,0:T(8,128)S(1)} %copy-done.3, ...), custom_call_target="tpu_custom_call" | custom-call | flops 1358954496 | bytes 6291456 | tf_op jit(solution)/shard_map/pallas_call | solution.py:313
  52.0 0.7 %copy.14 = bf16[1,512,128]{2,1,0:T(8,128)(2,1)} copy(bf16[1,512,128]{2,1,0:T(8,128)(2,1)S(1)} %get-tuple-element.6) | data formatting | bytes 262144
  52.6 0.7 %copy.15 = bf16[1,512,128]{2,1,0:T(8,128)(2,1)} copy(bf16[1,512,128]{2,1,0:T(8,128)(2,1)S(1)} %get-tuple-element.7) | data formatting | bytes 262144
  53.3 1.2 %copy.16 = f32[3456,128]{1,0:T(8,128)} copy(f32[3456,128]{1,0:T(8,128)S(1)} %get-tuple-element.8) | data formatting | bytes 3538944
Async XLA Ops:
  1.3 1.2 %copy-start = (bf16[3456,128]{1,0:T(8,128)(2,1)S(1)}, bf16[3456,128]{1,0:T(8,128)(2,1)}, u32[]{:S(2)}) copy-start(bf16[3456,128]{1,0:T(8,128)(2,1)} %ker.1) | copy-start | bytes 2654212
  2.4 0.9 %copy-start.1 = (bf16[1,512,128]{2,1,0:T(8,128)(2,1)S(1)}, bf16[1,512,128]{2,1,0:T(8,128)(2,1)}, u32[]{:S(2)}) copy-start(bf16[1,512,128]{2,1,0:T(8,128)(2,1)} %feat.1) | copy-start | bytes 393220
  3.4 0.9 %copy-start.2 = (bf16[1,512,128]{2,1,0:T(8,128)(2,1)S(1)}, bf16[1,512,128]{2,1,0:T(8,128)(2,1)}, u32[]{:S(2)}) copy-start(bf16[1,512,128]{2,1,0:T(8,128)(2,1)} %cot.1) | copy-start | bytes 393220
  4.3 0.7 %copy-start.3 = (s32[1,8,27]{2,1,0:T(8,128)S(1)}, s32[1,8,27]{2,1,0:T(8,128)}, u32[]{:S(2)}) copy-start(s32[1,8,27]{2,1,0:T(8,128)} %pairs_v.1) | copy-start | bytes 2596
  4.9 0.7 %copy-start.4 = (s32[1,512]{1,0:T(1,128)S(1)}, s32[1,512]{1,0:T(1,128)}, u32[]{:S(2)}) copy-start(s32[1,512]{1,0:T(1,128)} %occ.1) | copy-start | bytes 6148
  5.6 0.7 %copy-start.5 = (s32[1,1,16]{2,1,0:T(1,128)S(1)}, s32[1,1,16]{2,1,0:T(1,128)}, u32[]{:S(2)}) copy-start(s32[1,1,16]{2,1,0:T(1,128)} %sends.1) | copy-start | bytes 196

commit v2 on v1

--- a/solution.py
+++ b/solution.py
@@ -12,6 +12,7 @@
 MESH = pl.DeviceIdType.MESH
 VOXELS = 64
 TAPS = 27
+VMEM_GRANT = 64 * 2**20 - 2**16
 
 
 def axis_places(step):
@@ -40,8 +41,9 @@
     return classes
 
 
-def kernel_body(sizes, scale, feat, occ, pairs_s, pairs_v, sends, weight, ker, cot,
-                out_f, out_g, out_k,
+def kernel_body(sizes, scale, feat_h, occ_h, pairs_h, sends_h, weight_h, ker_h, cot_h,
+                home_f, home_g, home_k, out_f, out_g, out_k,
+                feat, occ, pairs_s, pairs_v, sends, weight, ker, cot, load_sem,
                 mask, fnat, table, gnat, gvox, patch, pgrad, cols, tgrad, conv, wgrad,
                 halo_out, halo_in, back_out, back_in, wsend, wrecv,
                 core_in, half_in, tail_in, tail_sum, send_sem, recv_sem):
@@ -56,6 +58,14 @@
 
     def peer_index(bit):
         return index[bit[0]] + (1 - 2 * bit_of(bit)) * (1 << bit[1])
+
+    loads = {}
+    for n, (name, src, dst) in enumerate([
+            ("occ", occ_h, occ), ("feat", feat_h, feat), ("sends", sends_h, sends),
+            ("weight", weight_h, weight), ("cot", cot_h, cot), ("pairs_s", pairs_h, pairs_s),
+            ("pairs_v", pairs_h, pairs_v), ("ker", ker_h, ker)]):
+        loads[name] = pltpu.make_async_copy(src, dst, load_sem.at[n])
+        loads[name].start()
 
     all_bits = [("dp", i) for i in range(ld)] + [("space", i) for i in range(ls)]
     barrier = pltpu.get_barrier_semaphore()
@@ -74,13 +84,17 @@
         started.append(copy)
         return copy
 
+    loads["occ"].wait()
     for i in range(own // 128):
         row = occ[0:1, i * 128:(i + 1) * 128].astype(jnp.float32)
         mask[i * 128:(i + 1) * 128, :] = jnp.transpose(jnp.broadcast_to(row, (128, 128)))
+    loads["feat"].wait()
     fnat[...] = feat[0].astype(jnp.float32) * mask[...]
     table[0:bricks] = fnat[...].reshape(bricks, VOXELS, chan)
     table[bricks + nspace * cap] = jnp.zeros((VOXELS, chan), jnp.float32)
 
+    loads["sends"].wait()
+    loads["weight"].wait()
     picks = []
     for level in range(ls):
         partner = peer_index(("space", level))
@@ -100,10 +114,12 @@
                  ("space", level)) for level in range(ls)]
     wcopy = send(wsend.at[0], wrecv.at[0], ("dp", 0))
 
+    loads["cot"].wait()
     gnat[...] = cot[0].astype(jnp.float32) * mask[...]
     for v in range(VOXELS):
         gvox[v * 8:(v + 1) * 8, :] = gnat[pl.ds(v, bricks, stride=VOXELS), :]
     grad = gvox[...].astype(jnp.bfloat16)
+    grad_t = jnp.transpose(gvox[...]).astype(jnp.bfloat16)
     for pos, v in slab(13):
         patch[pos[0], pos[1], pos[2]] = fnat[pl.ds(v, bricks, stride=VOXELS), :]
     pgrad[...] = jnp.zeros(pgrad.shape, jnp.float32)
@@ -115,6 +131,7 @@
                                    (((1,), (1,)), ((), ())), preferred_element_type=jnp.float32)
             pgrad[a:a + 4, b:b + 4, c:c + 4] += part.reshape(4, 4, 4, bricks, chan)
 
+    loads["ker"].wait()
     spread(range(0, 9))
 
     for level in range(ls):
@@ -128,6 +145,7 @@
         wsend[level + 1] = wsend[level] + wrecv[level]
         if level + 1 < ld:
             wcopy = send(wsend.at[level + 1], wrecv.at[level + 1], ("dp", level + 1))
+    loads["pairs_s"].wait()
     for b in range(bricks):
         for offset in range(TAPS):
             if offset != 13:
@@ -150,63 +168,68 @@
 
     def weigh(taps):
         lo, hi = taps[0] * chan, (taps[-1] + 1) * chan
-        wgrad[lo:hi, :] = own_weight * lax.dot_general(
-            cols[:, lo:hi], grad, (((0,), (0,)), ((), ())), preferred_element_type=jnp.float32)
+        turned = own_weight * jnp.dot(grad_t, cols[:, lo:hi], preferred_element_type=jnp.float32)
+        for n, tap in enumerate(taps):
+            wgrad[tap * chan:(tap + 1) * chan, :] = turned[:, n * chan:(n + 1) * chan]
 
     def tile8(x):
         return pl.multiple_of(x, 8)
 
-    cores = []
-    done = 0
+    units = part_rows // 64
+    sizes_of = [(units + 1) // 2 * 64, units // 2 * 64]
+    starts_of = [0, sizes_of[0]]
+    offs = {(p, s): mine * half_rows + p * part_rows + starts_of[s]
+            for s in range(2) for p in range(3)}
+    flight = {}
+    low_at, high_at = 0, half_rows // chan
     for p in range(3):
-        low_end = -(-(p + 1) * part_rows // chan)
-        mid = half_rows // chan
+        low_end = min(-(-(p + 1) * part_rows // chan), half_rows // chan)
         high_end = -(-(half_rows + (p + 1) * part_rows) // chan)
-        low_end = min(low_end, mid)
-        if p == 0:
-            low_at, high_at = 0, mid
-        if low_end > low_at:
-            weigh(list(range(low_at, low_end)))
+        weigh(list(range(low_at, low_end)))
         weigh(list(range(high_at, high_end)))
         low_at, high_at = low_end, high_end
-        src = tile8((1 - mine) * half_rows + p * part_rows)
-        cores.append(send(wgrad.at[pl.ds(src, part_rows)], core_in.at[p], first))
-
-    offs = [mine * half_rows + p * part_rows for p in range(3)]
-    flight = list(cores)
-    width = part_rows
-
-    def reduce_stage(j):
+        for s in range(2):
+            src = tile8((1 - mine) * half_rows + p * part_rows + starts_of[s])
+            flight[p, s] = send(wgrad.at[pl.ds(src, sizes_of[s])],
+                                core_in.at[p, pl.ds(starts_of[s], sizes_of[s])], first)
+
+    def reduce_stage(j, s):
         for p in range(3):
-            flight[p].wait_recv()
-            size = part_rows >> min(j, 3)
-            off = tile8(offs[p])
+            flight[p, s].wait_recv()
+            size = sizes_of[s] >> min(j, 3)
+            off = tile8(offs[p, s])
+            tail_at = starts_of[s] >> 3
             if j == 0:
-                wgrad[pl.ds(off, size), :] += core_in[p]
+                wgrad[pl.ds(off, size), :] += core_in[p, starts_of[s]:starts_of[s] + size, :]
             elif j <= 3:
-                at = part_rows - (part_rows >> (j - 1))
+                at = starts_of[s] + sizes_of[s] - (sizes_of[s] >> (j - 1))
                 wgrad[pl.ds(off, size), :] += half_in[p, at:at + size, :]
             else:
                 i = j - 4
-                held = wgrad[pl.ds(off, size), :] if i == 0 else tail_sum[p, i - 1]
-                tail_sum[p, i] = held + tail_in[p, i]
+                held = (wgrad[pl.ds(off, size), :] if i == 0
+                        else tail_sum[p, i - 1, tail_at:tail_at + size, :])
+                tail_sum[p, i, tail_at:tail_at + size, :] = (
+                    held + tail_in[p, i, tail_at:tail_at + size, :])
             if j < 3:
                 bit = orders[p][j]
                 half = size // 2
-                at = part_rows - (part_rows >> j)
-                other = tile8(offs[p] + (1 - bit_of(bit)) * half)
-                flight[p] = send(wgrad.at[pl.ds(other, half)],
-                                 half_in.at[p, pl.ds(at, half)], bit)
-                offs[p] = offs[p] + bit_of(bit) * half
+                at = starts_of[s] + sizes_of[s] - (sizes_of[s] >> j)
+                other = tile8(offs[p, s] + (1 - bit_of(bit)) * half)
+                flight[p, s] = send(wgrad.at[pl.ds(other, half)],
+                                    half_in.at[p, pl.ds(at, half)], bit)
+                offs[p, s] = offs[p, s] + bit_of(bit) * half
             elif j - 3 < len(tail):
                 i = j - 3
-                src = wgrad.at[pl.ds(off, size)] if i == 0 else tail_sum.at[p, i - 1]
-                flight[p] = send(src, tail_in.at[p, i], tail[i])
-
-    reduce_stage(0)
+                src = (wgrad.at[pl.ds(off, size)] if i == 0
+                       else tail_sum.at[p, i - 1, pl.ds(tail_at, size)])
+                flight[p, s] = send(src, tail_in.at[p, i, pl.ds(tail_at, size)], tail[i])
+
     spread(range(9, 18))
-    reduce_stage(1)
+    reduce_stage(0, 0)
+    reduce_stage(0, 1)
     spread(range(18, 27))
+    reduce_stage(1, 0)
+    reduce_stage(1, 1)
 
     entries = tgrad.shape[0] // VOXELS
     lane = lax.broadcasted_iota(jnp.int32, (1, 128), 1)
@@ -215,11 +238,14 @@
         for k in range(cap):
             name = bricks + peer_index(("space", level)) * cap + k
             code = jnp.where(lane == bricks + level * cap + k, name, code)
+    loads["pairs_v"].wait()
     hits = {}
     for offset in range(TAPS):
         hit = pairs_v[0, :, offset:offset + 1] == code
         hits[offset] = jnp.where(hit, 1.0, 0.0).astype(jnp.float32)
-    for offsets, voxels in voxel_classes().items():
+    for turn_of, (offsets, voxels) in enumerate(voxel_classes().items()):
+        if turn_of == 14:
+            reduce_stage(2, 0)
         left = jnp.concatenate([hits[o] for o in offsets] * 2, axis=0).astype(jnp.bfloat16)
         right = jnp.concatenate(
             [jnp.concatenate([pgrad[pos[j][0], pos[j][1], pos[j][2]] for _, pos in voxels], axis=1)
@@ -236,64 +262,109 @@
     back = [send(back_out.at[pl.ds(level * rows, rows)], back_in.at[pl.ds(level * rows, rows)],
                  ("space", level)) for level in range(ls)]
 
-    reduce_stage(2)
+    reduce_stage(2, 1)
     third = TAPS // 3 * chan
 
     def convolve(i):
         return jnp.dot(cols[:, i * third:(i + 1) * third], ker[i * third:(i + 1) * third, :],
                        preferred_element_type=jnp.float32)
 
+    total = wsend[ld][0:1, :]
+    kernel_scale = (ndp / total) * scale
+
+    def gather_start(j, s):
+        for p in range(3):
+            size = sizes_of[s] >> j
+            off = tile8(offs[p, s])
+            bit = orders[p][j - 1] if j else first
+            flight[p, s] = send(out_k.at[pl.ds(off, size)], out_k.at[pl.ds(off, size)], bit)
+            if j:
+                offs[p, s] = offs[p, s] - bit_of(bit) * size
+
+    def gather_wait(s):
+        for p in range(3):
+            flight[p, s].wait_recv()
+
+    def finish(s):
+        for j in range(len(tail)):
+            reduce_stage(4 + j, s)
+        last = sizes_of[s] >> 3
+        tail_at = starts_of[s] >> 3
+        for p in range(3):
+            off = tile8(offs[p, s])
+            held = (tail_sum[p, len(tail) - 1, tail_at:tail_at + last, :] if tail
+                    else wgrad[pl.ds(off, last), :])
+            out_k[pl.ds(off, last), :] = held * kernel_scale
+        gather_start(3, s)
+
     conv[...] = convolve(0) + patch[1:5, 1:5, 1:5].reshape(own, chan)
-    reduce_stage(3)
+    reduce_stage(3, 0)
     conv[...] += convolve(1)
-    for j in range(len(tail)):
-        reduce_stage(4 + j)
-    total = wsend[ld][0:1, :]
-    last = part_rows >> 3
-    kernel_scale = (ndp / total) * scale
-    for p in range(3):
-        off = tile8(offs[p])
-        held = tail_sum[p, len(tail) - 1] if tail else wgrad[pl.ds(off, last), :]
-        out_k[pl.ds(off, last), :] = held * kernel_scale
-
-    def gather_start(j):
-        for p in range(3):
-            size = part_rows >> j
-            off = tile8(offs[p])
-            bit = orders[p][j - 1] if j else first
-            flight[p] = send(out_k.at[pl.ds(off, size)], out_k.at[pl.ds(off, size)], bit)
-            if j:
-                offs[p] = offs[p] - bit_of(bit) * size
-
-    def gather_wait():
-        for p in range(3):
-            flight[p].wait_recv()
-
-    gather_start(3)
+    reduce_stage(3, 1)
     conv[...] += convolve(2)
-    gather_wait()
-    gather_start(2)
     for v in range(VOXELS):
         gvox[pl.ds(v, bricks, stride=VOXELS), :] = conv[v * 8:(v + 1) * 8, :]
     out_f[0] = (gvox[...] * mask[...]).astype(jnp.bfloat16)
-    gather_wait()
-    gather_start(1)
+    homes = [pltpu.make_async_copy(out_f, home_f, load_sem.at[8])]
+    homes[0].start()
+    finish(0)
     for copy in back:
         copy.wait_recv()
     factor = own_weight * ndp / total
-    for b in range(bricks):
-        lo, hi = b * VOXELS, (b + 1) * VOXELS
-        held = gnat[lo:hi, :] + tgrad[lo:hi, :]
-        for e, chosen in enumerate(picks):
-            came = back_in[e * VOXELS:(e + 1) * VOXELS, :].astype(jnp.float32)
-            here = jnp.full((VOXELS, chan), chosen, jnp.int32) == b
-            held = held + jnp.where(here, came, 0.0)
-        out_g[0, lo:hi, :] = (factor * (mask[lo:hi, :] * held)).astype(jnp.bfloat16)
-    gather_wait()
-    gather_start(0)
-    gather_wait()
+
+    def feature_grads(some):
+        for b in some:
+            lo, hi = b * VOXELS, (b + 1) * VOXELS
+            held = gnat[lo:hi, :] + tgrad[lo:hi, :]
+            for e, chosen in enumerate(picks):
+                came = back_in[e * VOXELS:(e + 1) * VOXELS, :].astype(jnp.float32)
+                here = jnp.full((VOXELS, chan), chosen, jnp.int32) == b
+                held = held + jnp.where(here, came, 0.0)
+            out_g[0, lo:hi, :] = (factor * (mask[lo:hi, :] * held)).astype(jnp.bfloat16)
+
+    feature_grads(range(bricks // 2))
+    finish(1)
+    feature_grads(range(bricks // 2, bricks))
+    homes.append(pltpu.make_async_copy(out_g, home_g, load_sem.at[9]))
+    homes[1].start()
+    for j in (2, 1, 0):
+        for s in range(2):
+            gather_wait(s)
+            gather_start(j, s)
+    for n, half in enumerate((mine, 1 - mine)):
+        if n == 1:
+            gather_wait(0)
+            gather_wait(1)
+        at = pl.ds(tile8(half * half_rows), half_rows)
+        homes.append(pltpu.make_async_copy(out_k.at[at], home_k.at[at], load_sem.at[10 + n]))
+        homes[-1].start()
+    for copy in homes:
+        copy.wait()
     for copy in started:
         copy.wait_send()
+
+
+def write_out(in_f, in_g, in_k, out_f, out_g, out_k, held, turned, sems):
+    chan = in_k.shape[1]
+    copies = [pltpu.make_async_copy(in_f, out_f, sems.at[0]),
+              pltpu.make_async_copy(in_g, out_g, sems.at[1])]
+    loads = []
+    for n in range(3):
+        at = pl.ds(n * TAPS // 3 * chan, TAPS // 3 * chan)
+        loads.append(pltpu.make_async_copy(in_k.at[at], held.at[at], sems.at[2 + n]))
+    for copy in loads + copies:
+        copy.start()
+    for n in range(3):
+        lo, hi = n * TAPS // 3, (n + 1) * TAPS // 3
+        loads[n].wait()
+        for tap in range(lo, hi):
+            at = slice(tap * chan, (tap + 1) * chan)
+            turned[at, :] = jnp.transpose(held[at, :])
+        at = pl.ds(lo * chan, (hi - lo) * chan)
+        copies.append(pltpu.make_async_copy(turned.at[at], out_k.at[at], sems.at[5 + n]))
+        copies[-1].start()
+    for copy in copies:
+        copy.wait()
 
 
 def on_device(features, occupancy, brick_pairs, send_lists, scan_weight, kernel, cotangent):
@@ -306,20 +377,33 @@
     rows = TAPS * chan
     part = rows // 6
     tail = max(ls + ld - 4, 1)
-    copies = 2 * ls + ld + 3 * (1 + 3 + (ls + ld - 4) + 4)
+    copies = 2 * ls + ld + 6 * (1 + 3 + (ls + ld - 4) + 4)
     f32, bf16 = jnp.float32, jnp.bfloat16
-    vmem, smem = pl.BlockSpec(memory_space=pltpu.VMEM), pl.BlockSpec(memory_space=pltpu.SMEM)
+    i32 = jnp.int32
+    hbm = pl.BlockSpec(memory_space=pltpu.HBM)
     scale = 1.0 / math.sqrt(64.0 * bricks * nspace)
-    return pl.pallas_call(
+    results = pl.pallas_call(
         functools.partial(kernel_body, (nspace, ndp, cap, bricks, chan), scale),
         out_shape=(
             jax.ShapeDtypeStruct(features.shape, bf16),
             jax.ShapeDtypeStruct(features.shape, bf16),
             jax.ShapeDtypeStruct((rows, chan), f32),
         ),
-        in_specs=[vmem, vmem, smem, vmem, smem, smem, vmem, vmem],
-        out_specs=(vmem, vmem, vmem),
+        in_specs=[hbm] * 7,
+        out_specs=(hbm, hbm, hbm),
         scratch_shapes=[
+            pltpu.VMEM(features.shape, bf16),
+            pltpu.VMEM(features.shape, bf16),
+            pltpu.VMEM((rows, chan), f32),
+            pltpu.VMEM(features.shape, bf16),
+            pltpu.VMEM(occupancy.shape, i32),
+            pltpu.SMEM(brick_pairs.shape, i32),
+            pltpu.VMEM(brick_pairs.shape, i32),
+            pltpu.SMEM(send_lists.shape, i32),
+            pltpu.SMEM(scan_weight.shape, i32),
+            pltpu.VMEM(kernel.shape, bf16),
+            pltpu.VMEM(cotangent.shape, bf16),
+            pltpu.SemaphoreType.DMA((12,)),
             pltpu.VMEM((own, chan), f32),
             pltpu.VMEM((own, chan), f32),
             pltpu.VMEM((bricks + nspace * cap + 1, VOXELS, chan), f32),
@@ -345,11 +429,21 @@
             pltpu.SemaphoreType.DMA((copies,)),
         ],
         compiler_params=pltpu.CompilerParams(
-            collective_id=0, has_side_effects=True, vmem_limit_bytes=50 * 1024 * 1024
+            collective_id=0, has_side_effects=True, vmem_limit_bytes=VMEM_GRANT
         ),
         cost_estimate=pl.CostEstimate(flops=6 * own * rows * chan, bytes_accessed=6 * 2**20,
                                       transcendentals=0),
-    )(features, occupancy, brick_pairs, brick_pairs, send_lists, scan_weight, kernel, cotangent)
+    )(features, occupancy, brick_pairs, send_lists, scan_weight, kernel, cotangent)
+    return pl.pallas_call(
+        write_out,
+        out_shape=tuple(jax.ShapeDtypeStruct(r.shape, r.dtype) for r in results),
+        in_specs=[hbm] * 3,
+        out_specs=(hbm, hbm, hbm),
+        scratch_shapes=[pltpu.VMEM((rows, chan), f32), pltpu.VMEM((rows, chan), f32),
+                        pltpu.SemaphoreType.DMA((8,))],
+        compiler_params=pltpu.CompilerParams(vmem_limit_bytes=VMEM_GRANT),
+        cost_estimate=pl.CostEstimate(flops=0, bytes_accessed=4 * 2**20, transcendentals=0),
+    )(*results)
 
 
 def solution(mesh):

time: 54.8 us -> 54.5 us (level)
  local copies, waits for them, and re-layouts: 7.51 us -> 0 us
  Pallas kernels: 45.7 us -> 53.1 us
    pallas_call x0 -> x1, Pallas kernels: none -> 9.12 us  [on_device(): pl.pallas_call(write_out, out_shape=tuple((jax.ShapeDtypeStruct(r.shape,...]
    unnamed x15 -> x0, local copies, waits for them, and re-layouts: 7.51 us -> none
    pallas_call x1, Pallas kernels: 45.7 us -> 44 us  [on_device(): pl.pallas_call(functools.partial(kernel_body, (nspace, ndp, cap, bricks,...]
where the time goes in v2:
time: 54.5 us; the launch traced here: 54.4 us
  Pallas kernels  53.1 us (97%)
  between operations  1.29 us (2%)
    pallas_call x1, Pallas kernels, on_device(): pl.pallas_call(functools.partial(kernel_body, (nspace, ndp, cap, bricks,...  44 us
    pallas_call x1, Pallas kernels, on_device(): pl.pallas_call(write_out, out_shape=tuple((jax.ShapeDtypeStruct(r.shape,...  9.12 us

profile of v2, /device:TPU:1, one launch (start us, length us, event | category | flops | bytes accessed | tf_op | source)
XLA Modules:
  0.0 54.4 jit_solution(206041301402868905)
XLA Ops:
  1.3 44.0 %shard_map.94 = (bf16[1,512,128]{2,1,0:T(8,128)(2,1)}, bf16[1,512,128]{2,1,0:T(8,128)(2,1)}, f32[3456,128]{1,0:T(8,128)}) custom-call(bf16[1,512,128]{2,1,0:T(8,128)(2,1)} %feat_h.1, s32[1,512]{1,0:T(1,128)} %occ_h.1, s32[1,8,27]{2,1,0:T(8,128)} %pairs_h.1, s32[1,1,16]{2,1,0:T(1,128)} %sends_h.1, s32[1]{0:T(128)S(6)} %copy.10.weight_h, ...), custom_call_target="tpu_custom_call" | custom-call | flops 1358954496 | bytes 6291456 | tf_op jit(solution)/shard_map/pallas_call | solution.py:385
  45.2 9.1 %shard_map.95 = (bf16[1,512,128]{2,1,0:T(8,128)(2,1)}, bf16[1,512,128]{2,1,0:T(8,128)(2,1)}, f32[3456,128]{1,0:T(8,128)}) custom-call(bf16[1,512,128]{2,1,0:T(8,128)(2,1)} %get-tuple-element.6.in_f, bf16[1,512,128]{2,1,0:T(8,128)(2,1)} %get-tuple-element.7.in_g, f32[3456,128]{1,0:T(8,128)} %get-tuple-element.8.in_k), custom_call_target="tpu_custom_call" | custom-call | bytes 4194304 | tf_op jit(solution)/shard_map/pallas_call | solution.py:437

commit v3 on v2

--- a/solution.py
+++ b/solution.py
@@ -119,7 +119,6 @@
     for v in range(VOXELS):
         gvox[v * 8:(v + 1) * 8, :] = gnat[pl.ds(v, bricks, stride=VOXELS), :]
     grad = gvox[...].astype(jnp.bfloat16)
-    grad_t = jnp.transpose(gvox[...]).astype(jnp.bfloat16)
     for pos, v in slab(13):
         patch[pos[0], pos[1], pos[2]] = fnat[pl.ds(v, bricks, stride=VOXELS), :]
     pgrad[...] = jnp.zeros(pgrad.shape, jnp.float32)
@@ -168,9 +167,8 @@
 
     def weigh(taps):
         lo, hi = taps[0] * chan, (taps[-1] + 1) * chan
-        turned = own_weight * jnp.dot(grad_t, cols[:, lo:hi], preferred_element_type=jnp.float32)
-        for n, tap in enumerate(taps):
-            wgrad[tap * chan:(tap + 1) * chan, :] = turned[:, n * chan:(n + 1) * chan]
+        wgrad[lo:hi, :] = own_weight * lax.dot_general(
+            cols[:, lo:hi], grad, (((0,), (0,)), ((), ())), preferred_element_type=jnp.float32)
 
     def tile8(x):
         return pl.multiple_of(x, 8)
@@ -181,20 +179,8 @@
     offs = {(p, s): mine * half_rows + p * part_rows + starts_of[s]
             for s in range(2) for p in range(3)}
     flight = {}
-    low_at, high_at = 0, half_rows // chan
-    for p in range(3):
-        low_end = min(-(-(p + 1) * part_rows // chan), half_rows // chan)
-        high_end = -(-(half_rows + (p + 1) * part_rows) // chan)
-        weigh(list(range(low_at, low_end)))
-        weigh(list(range(high_at, high_end)))
-        low_at, high_at = low_end, high_end
-        for s in range(2):
-            src = tile8((1 - mine) * half_rows + p * part_rows + starts_of[s])
-            flight[p, s] = send(wgrad.at[pl.ds(src, sizes_of[s])],
-                                core_in.at[p, pl.ds(starts_of[s], sizes_of[s])], first)
-
-    def reduce_stage(j, s):
-        for p in range(3):
+    def reduce_stage(j, s, parts=range(3)):
+        for p in parts:
             flight[p, s].wait_recv()
             size = sizes_of[s] >> min(j, 3)
             off = tile8(offs[p, s])
@@ -224,12 +210,31 @@
                        else tail_sum.at[p, i - 1, pl.ds(tail_at, size)])
                 flight[p, s] = send(src, tail_in.at[p, i, pl.ds(tail_at, size)], tail[i])
 
-    spread(range(9, 18))
-    reduce_stage(0, 0)
-    reduce_stage(0, 1)
-    spread(range(18, 27))
+    for p in range(3):
+        if p > 1:
+            reduce_stage(0, 0, [p - 2])
+            reduce_stage(0, 1, [p - 2])
+        low_at = min(-(-p * part_rows // chan), half_rows // chan)
+        high_at = -(-(half_rows + p * part_rows) // chan) if p else half_rows // chan
+        low_end = min(-(-(p + 1) * part_rows // chan), half_rows // chan)
+        high_end = -(-(half_rows + (p + 1) * part_rows) // chan)
+        weigh(list(range(low_at, low_end)))
+        weigh(list(range(high_at, high_end)))
+        for s in range(2):
+            src = tile8((1 - mine) * half_rows + p * part_rows + starts_of[s])
+            flight[p, s] = send(wgrad.at[pl.ds(src, sizes_of[s])],
+                                core_in.at[p, pl.ds(starts_of[s], sizes_of[s])], first)
+
+    reduce_stage(0, 0, [1])
+    reduce_stage(0, 1, [1])
+    spread(range(9, 13))
+    reduce_stage(0, 0, [2])
+    reduce_stage(0, 1, [2])
+    spread(range(13, 18))
     reduce_stage(1, 0)
+    spread(range(18, 23))
     reduce_stage(1, 1)
+    spread(range(23, 27))
 
     entries = tgrad.shape[0] // VOXELS
     lane = lax.broadcasted_iota(jnp.int32, (1, 128), 1)
@@ -344,26 +349,22 @@
         copy.wait_send()
 
 
-def write_out(in_f, in_g, in_k, out_f, out_g, out_k, held, turned, sems):
-    chan = in_k.shape[1]
-    copies = [pltpu.make_async_copy(in_f, out_f, sems.at[0]),
-              pltpu.make_async_copy(in_g, out_g, sems.at[1])]
-    loads = []
-    for n in range(3):
-        at = pl.ds(n * TAPS // 3 * chan, TAPS // 3 * chan)
-        loads.append(pltpu.make_async_copy(in_k.at[at], held.at[at], sems.at[2 + n]))
-    for copy in loads + copies:
+def write_out(in_f, in_g, in_k, out_f, out_g, out_k, held_f, held_g, held_k, sems):
+    rows = in_k.shape[0] // 4
+    moves = [(in_f, held_f, out_f), (in_g, held_g, out_g)]
+    for n in range(4):
+        at = pl.ds(n * rows, rows)
+        moves.append((in_k.at[at], held_k.at[at], out_k.at[at]))
+    loads = [pltpu.make_async_copy(src, held, sems.at[2 * n])
+             for n, (src, held, _) in enumerate(moves)]
+    for copy in loads:
         copy.start()
-    for n in range(3):
-        lo, hi = n * TAPS // 3, (n + 1) * TAPS // 3
-        loads[n].wait()
-        for tap in range(lo, hi):
-            at = slice(tap * chan, (tap + 1) * chan)
-            turned[at, :] = jnp.transpose(held[at, :])
-        at = pl.ds(lo * chan, (hi - lo) * chan)
-        copies.append(pltpu.make_async_copy(turned.at[at], out_k.at[at], sems.at[5 + n]))
-        copies[-1].start()
-    for copy in copies:
+    stores = [pltpu.make_async_copy(held, dst, sems.at[2 * n + 1])
+              for n, (_, held, dst) in enumerate(moves)]
+    for load, store in zip(loads, stores):
+        load.wait()
+        store.start()
+    for copy in stores:
         copy.wait()
 
 
@@ -439,8 +440,8 @@
         out_shape=tuple(jax.ShapeDtypeStruct(r.shape, r.dtype) for r in results),
         in_specs=[hbm] * 3,
         out_specs=(hbm, hbm, hbm),
-        scratch_shapes=[pltpu.VMEM((rows, chan), f32), pltpu.VMEM((rows, chan), f32),
-                        pltpu.SemaphoreType.DMA((8,))],
+        scratch_shapes=[pltpu.VMEM(features.shape, bf16), pltpu.VMEM(features.shape, bf16),
+                        pltpu.VMEM((rows, chan), f32), pltpu.SemaphoreType.DMA((12,))],
         compiler_params=pltpu.CompilerParams(vmem_limit_bytes=VMEM_GRANT),
         cost_estimate=pl.CostEstimate(flops=0, bytes_accessed=4 * 2**20, transcendentals=0),
     )(*results)

time: 54.5 us -> 48 us (0.88)
  Pallas kernels: 53.1 us -> 46.6 us
    pallas_call x1, Pallas kernels: 9.12 us -> 2.45 us  [on_device(): pl.pallas_call(write_out, out_shape=tuple((jax.ShapeDtypeStruct(r.shape,...]
where the time goes in v3:
time: 48 us; the launch traced here: 47.9 us
  Pallas kernels  46.6 us (97%)
  between operations  1.29 us (3%)
    pallas_call x1, Pallas kernels, on_device(): pl.pallas_call(functools.partial(kernel_body, (nspace, ndp, cap, bricks,...  44.1 us
    pallas_call x1, Pallas kernels, on_device(): pl.pallas_call(write_out, out_shape=tuple((jax.ShapeDtypeStruct(r.shape,...  2.45 us

profile of v3, /device:TPU:1, one launch (start us, length us, event | category | flops | bytes accessed | tf_op | source)
XLA Modules:
  0.0 47.9 jit_solution(10333804583195899134)
XLA Ops:
  1.3 44.1 %shard_map.94 = (bf16[1,512,128]{2,1,0:T(8,128)(2,1)}, bf16[1,512,128]{2,1,0:T(8,128)(2,1)}, f32[3456,128]{1,0:T(8,128)}) custom-call(bf16[1,512,128]{2,1,0:T(8,128)(2,1)} %feat_h.1, s32[1,512]{1,0:T(1,128)} %occ_h.1, s32[1,8,27]{2,1,0:T(8,128)} %pairs_h.1, s32[1,1,16]{2,1,0:T(1,128)} %sends_h.1, s32[1]{0:T(128)S(6)} %copy.10.weight_h, ...), custom_call_target="tpu_custom_call" | custom-call | flops 1358954496 | bytes 6291456 | tf_op jit(solution)/shard_map/pallas_call | solution.py:386
  45.4 2.5 %shard_map.95 = (bf16[1,512,128]{2,1,0:T(8,128)(2,1)}, bf16[1,512,128]{2,1,0:T(8,128)(2,1)}, f32[3456,128]{1,0:T(8,128)}) custom-call(bf16[1,512,128]{2,1,0:T(8,128)(2,1)} %get-tuple-element.6.in_f, bf16[1,512,128]{2,1,0:T(8,128)(2,1)} %get-tuple-element.7.in_g, f32[3456,128]{1,0:T(8,128)} %get-tuple-element.8.in_k), custom_call_target="tpu_custom_call" | custom-call | bytes 4194304 | tf_op jit(solution)/shard_map/pallas_call | solution.py:438

commit v4 on v3

--- a/solution.py
+++ b/solution.py
@@ -43,7 +43,7 @@
 
 def kernel_body(sizes, scale, feat_h, occ_h, pairs_h, sends_h, weight_h, ker_h, cot_h,
                 home_f, home_g, home_k, out_f, out_g, out_k,
-                feat, occ, pairs_s, pairs_v, sends, weight, ker, cot, load_sem,
+                feat, occ, pairs_s, pairs_v, sends, weight, ker, cot, load_sem, gcols,
                 mask, fnat, table, gnat, gvox, patch, pgrad, cols, tgrad, conv, wgrad,
                 halo_out, halo_in, back_out, back_in, wsend, wrecv,
                 core_in, half_in, tail_in, tail_sum, send_sem, recv_sem):
@@ -123,15 +123,26 @@
         patch[pos[0], pos[1], pos[2]] = fnat[pl.ds(v, bricks, stride=VOXELS), :]
     pgrad[...] = jnp.zeros(pgrad.shape, jnp.float32)
 
-    def spread(taps):
-        for tap in taps:
-            a, b, c = tap // 9, tap // 3 % 3, tap % 3
-            part = lax.dot_general(grad, ker[tap * chan:(tap + 1) * chan, :],
-                                   (((1,), (1,)), ((), ())), preferred_element_type=jnp.float32)
-            pgrad[a:a + 4, b:b + 4, c:c + 4] += part.reshape(4, 4, 4, bricks, chan)
+    plane = own // 4
+    for px in range(6):
+        for a in range(3):
+            x = px - a
+            gcols[px * plane:(px + 1) * plane, a * chan:(a + 1) * chan] = (
+                grad[x * plane:(x + 1) * plane, :] if 0 <= x < 4
+                else jnp.zeros((plane, chan), jnp.bfloat16))
+
+    def spread(groups):
+        for group in groups:
+            b, c = group // 3, group % 3
+            taps = [9 * a + group for a in range(3)]
+            part = lax.dot_general(
+                gcols[...],
+                jnp.concatenate([ker[tap * chan:(tap + 1) * chan, :] for tap in taps], axis=1),
+                (((1,), (1,)), ((), ())), preferred_element_type=jnp.float32)
+            pgrad[:, b:b + 4, c:c + 4] += part.reshape(6, 4, 4, bricks, chan)
 
     loads["ker"].wait()
-    spread(range(0, 9))
+    spread(range(0, 3))
 
     for level in range(ls):
         halo[level].wait_recv()
@@ -152,11 +163,6 @@
                 for pos, v in slab(offset):
                     patch[pos[0], pos[1], pos[2], b:b + 1, :] = table[entry, v:v + 1, :]
 
-    for tap in range(TAPS):
-        a, b, c = tap // 9, tap // 3 % 3, tap % 3
-        cols[:, tap * chan:(tap + 1) * chan] = patch[a:a + 4, b:b + 4, c:c + 4].reshape(
-            own, chan).astype(jnp.bfloat16)
-
     total_rows = TAPS * chan
     half_rows = total_rows // 2
     part_rows = half_rows // 3
@@ -166,6 +172,10 @@
     mine = bit_of(first)
 
     def weigh(taps):
+        for tap in taps:
+            a, b, c = tap // 9, tap // 3 % 3, tap % 3
+            cols[:, tap * chan:(tap + 1) * chan] = patch[a:a + 4, b:b + 4, c:c + 4].reshape(
+                own, chan).astype(jnp.bfloat16)
         lo, hi = taps[0] * chan, (taps[-1] + 1) * chan
         wgrad[lo:hi, :] = own_weight * lax.dot_general(
             cols[:, lo:hi], grad, (((0,), (0,)), ((), ())), preferred_element_type=jnp.float32)
@@ -227,14 +237,14 @@
 
     reduce_stage(0, 0, [1])
     reduce_stage(0, 1, [1])
-    spread(range(9, 13))
+    spread(range(3, 5))
     reduce_stage(0, 0, [2])
     reduce_stage(0, 1, [2])
-    spread(range(13, 18))
+    spread(range(5, 6))
     reduce_stage(1, 0)
-    spread(range(18, 23))
+    spread(range(6, 8))
     reduce_stage(1, 1)
-    spread(range(23, 27))
+    spread(range(8, 9))
 
     entries = tgrad.shape[0] // VOXELS
     lane = lax.broadcasted_iota(jnp.int32, (1, 128), 1)
@@ -277,18 +287,31 @@
     total = wsend[ld][0:1, :]
     kernel_scale = (ndp / total) * scale
 
+    to_core = {(p, s): [] for p in range(3) for s in range(2)}
+
+    def to_other_core(p, s, off, size):
+        at = pl.ds(tile8(off), size)
+        to_core[p, s].append(send(out_k.at[at], out_k.at[at], first))
+
     def gather_start(j, s):
         for p in range(3):
             size = sizes_of[s] >> j
             off = tile8(offs[p, s])
-            bit = orders[p][j - 1] if j else first
+            bit = orders[p][j - 1]
             flight[p, s] = send(out_k.at[pl.ds(off, size)], out_k.at[pl.ds(off, size)], bit)
-            if j:
-                offs[p, s] = offs[p, s] - bit_of(bit) * size
-
-    def gather_wait(s):
+
+    def gather_take(j, s):
+        came = {}
         for p in range(3):
             flight[p, s].wait_recv()
+            size = sizes_of[s] >> j
+            bit = orders[p][j - 1]
+            came[p] = (offs[p, s] + (1 - 2 * bit_of(bit)) * size, size)
+            offs[p, s] = offs[p, s] - bit_of(bit) * size
+        if j > 1:
+            gather_start(j - 1, s)
+        for p in range(3):
+            to_other_core(p, s, *came[p])
 
     def finish(s):
         for j in range(len(tail)):
@@ -301,6 +324,8 @@
                     else wgrad[pl.ds(off, last), :])
             out_k[pl.ds(off, last), :] = held * kernel_scale
         gather_start(3, s)
+        for p in range(3):
+            to_other_core(p, s, offs[p, s], last)
 
     conv[...] = convolve(0) + patch[1:5, 1:5, 1:5].reshape(own, chan)
     reduce_stage(3, 0)
@@ -332,17 +357,21 @@
     feature_grads(range(bricks // 2, bricks))
     homes.append(pltpu.make_async_copy(out_g, home_g, load_sem.at[9]))
     homes[1].start()
-    for j in (2, 1, 0):
+    for j in (3, 2, 1):
         for s in range(2):
-            gather_wait(s)
-            gather_start(j, s)
-    for n, half in enumerate((mine, 1 - mine)):
-        if n == 1:
-            gather_wait(0)
-            gather_wait(1)
-        at = pl.ds(tile8(half * half_rows), half_rows)
-        homes.append(pltpu.make_async_copy(out_k.at[at], home_k.at[at], load_sem.at[10 + n]))
+            gather_take(j, s)
+
+    def go_home(off, size):
+        at = pl.ds(tile8(off), size)
+        homes.append(pltpu.make_async_copy(out_k.at[at], home_k.at[at], load_sem.at[8 + len(homes)]))
         homes[-1].start()
+
+    go_home(mine * half_rows, half_rows)
+    for s in range(2):
+        for p in range(3):
+            for copy in to_core[p, s]:
+                copy.wait_recv()
+            go_home((1 - mine) * half_rows + p * part_rows + starts_of[s], sizes_of[s])
     for copy in homes:
         copy.wait()
     for copy in started:
@@ -378,7 +407,7 @@
     rows = TAPS * chan
     part = rows // 6
     tail = max(ls + ld - 4, 1)
-    copies = 2 * ls + ld + 6 * (1 + 3 + (ls + ld - 4) + 4)
+    copies = 2 * ls + ld + 6 * (1 + 3 + (ls + ld - 4) + 3 + 4)
     f32, bf16 = jnp.float32, jnp.bfloat16
     i32 = jnp.int32
     hbm = pl.BlockSpec(memory_space=pltpu.HBM)
@@ -404,7 +433,8 @@
             pltpu.SMEM(scan_weight.shape, i32),
             pltpu.VMEM(kernel.shape, bf16),
             pltpu.VMEM(cotangent.shape, bf16),
-            pltpu.SemaphoreType.DMA((12,)),
+            pltpu.SemaphoreType.DMA((17,)),
+            pltpu.VMEM((own // 4 * 6, 3 * chan), bf16),
             pltpu.VMEM((own, chan), f32),
             pltpu.VMEM((own, chan), f32),
             pltpu.VMEM((bricks + nspace * cap + 1, VOXELS, chan), f32),

time: 48 us -> 47.6 us (level)
  Pallas kernels: 46.6 us -> 46.1 us
where the time goes in v4:
time: 47.6 us; the launch traced here: 47.4 us
  Pallas kernels  46.1 us (97%)
  between operations  1.29 us (3%)
    pallas_call x1, Pallas kernels, on_device(): pl.pallas_call(functools.partial(kernel_body, (nspace, ndp, cap, bricks,...  43.7 us
    pallas_call x1, Pallas kernels, on_device(): pl.pallas_call(write_out, out_shape=tuple((jax.ShapeDtypeStruct(r.shape,...  2.45 us

profile of v4, /device:TPU:1, one launch (start us, length us, event | category | flops | bytes accessed | tf_op | source)
XLA Modules:
  0.0 47.4 jit_solution(14712136847254693671)
XLA Ops:
  1.3 43.7 %shard_map.94 = (bf16[1,512,128]{2,1,0:T(8,128)(2,1)}, bf16[1,512,128]{2,1,0:T(8,128)(2,1)}, f32[3456,128]{1,0:T(8,128)}) custom-call(bf16[1,512,128]{2,1,0:T(8,128)(2,1)} %feat_h.1, s32[1,512]{1,0:T(1,128)} %occ_h.1, s32[1,8,27]{2,1,0:T(8,128)} %pairs_h.1, s32[1,1,16]{2,1,0:T(1,128)} %sends_h.1, s32[1]{0:T(128)S(6)} %copy.10.weight_h, ...), custom_call_target="tpu_custom_call" | custom-call | flops 1358954496 | bytes 6291456 | tf_op jit(solution)/shard_map/pallas_call | solution.py:415
  45.0 2.5 %shard_map.95 = (bf16[1,512,128]{2,1,0:T(8,128)(2,1)}, bf16[1,512,128]{2,1,0:T(8,128)(2,1)}, f32[3456,128]{1,0:T(8,128)}) custom-call(bf16[1,512,128]{2,1,0:T(8,128)(2,1)} %get-tuple-element.6.in_f, bf16[1,512,128]{2,1,0:T(8,128)(2,1)} %get-tuple-element.7.in_g, f32[3456,128]{1,0:T(8,128)} %get-tuple-element.8.in_k), custom_call_target="tpu_custom_call" | custom-call | bytes 4194304 | tf_op jit(solution)/shard_map/pallas_call | solution.py:468

commit v5 on v4

--- a/solution.py
+++ b/solution.py
@@ -39,6 +39,14 @@
         key = tuple(o for o, _ in readers[voxel])
         classes.setdefault(key, []).append((voxel, [pos for _, pos in readers[voxel]]))
     return classes
+
+
+def each(first, last, body):
+    lax.fori_loop(first, last, lambda i, carry: (body(i), carry)[1], 0)
+
+
+def tap_shifts(tap):
+    return lax.div(tap, 9), lax.rem(lax.div(tap, 3), 3), lax.rem(tap, 3)
 
 
 def kernel_body(sizes, scale, feat_h, occ_h, pairs_h, sends_h, weight_h, ker_h, cot_h,
@@ -131,18 +139,19 @@
                 grad[x * plane:(x + 1) * plane, :] if 0 <= x < 4
                 else jnp.zeros((plane, chan), jnp.bfloat16))
 
-    def spread(groups):
-        for group in groups:
-            b, c = group // 3, group % 3
-            taps = [9 * a + group for a in range(3)]
+    def spread(first, last):
+        def one(group):
+            b, c = lax.div(group, 3), lax.rem(group, 3)
+            rows_of = [pl.ds(pl.multiple_of((9 * a + group) * chan, chan), chan) for a in range(3)]
             part = lax.dot_general(
-                gcols[...],
-                jnp.concatenate([ker[tap * chan:(tap + 1) * chan, :] for tap in taps], axis=1),
+                gcols[...], jnp.concatenate([ker[at, :] for at in rows_of], axis=1),
                 (((1,), (1,)), ((), ())), preferred_element_type=jnp.float32)
-            pgrad[:, b:b + 4, c:c + 4] += part.reshape(6, 4, 4, bricks, chan)
+            pgrad[:, pl.ds(b, 4), pl.ds(c, 4)] += part.reshape(6, 4, 4, bricks, chan)
+
+        each(first, last, one)
 
     loads["ker"].wait()
-    spread(range(0, 3))
+    spread(0, 3)
 
     for level in range(ls):
         halo[level].wait_recv()
@@ -156,12 +165,15 @@
         if level + 1 < ld:
             wcopy = send(wsend.at[level + 1], wrecv.at[level + 1], ("dp", level + 1))
     loads["pairs_s"].wait()
-    for b in range(bricks):
+
+    def fill(b):
         for offset in range(TAPS):
             if offset != 13:
                 entry = pairs_s[0, b, offset]
                 for pos, v in slab(offset):
-                    patch[pos[0], pos[1], pos[2], b:b + 1, :] = table[entry, v:v + 1, :]
+                    patch[pos[0], pos[1], pos[2], pl.ds(b, 1), :] = table[entry, v:v + 1, :]
+
+    each(0, bricks, fill)
 
     total_rows = TAPS * chan
     half_rows = total_rows // 2
@@ -171,14 +183,18 @@
     orders = [[turn[(p + j) % 3] for j in range(3)] for p in range(3)]
     mine = bit_of(first)
 
-    def weigh(taps):
-        for tap in taps:
-            a, b, c = tap // 9, tap // 3 % 3, tap % 3
-            cols[:, tap * chan:(tap + 1) * chan] = patch[a:a + 4, b:b + 4, c:c + 4].reshape(
-                own, chan).astype(jnp.bfloat16)
-        lo, hi = taps[0] * chan, (taps[-1] + 1) * chan
-        wgrad[lo:hi, :] = own_weight * lax.dot_general(
-            cols[:, lo:hi], grad, (((0,), (0,)), ((), ())), preferred_element_type=jnp.float32)
+    def weigh(first_tap, last_tap):
+        def one(tap):
+            a, b, c = tap_shifts(tap)
+            at = pl.ds(pl.multiple_of(tap * chan, chan), chan)
+            column = patch[pl.ds(a, 4), pl.ds(b, 4), pl.ds(c, 4)].reshape(own, chan).astype(
+                jnp.bfloat16)
+            cols[:, at] = column
+            wgrad[at, :] = own_weight * lax.dot_general(
+                column, gcols[0:own, 0:chan], (((0,), (0,)), ((), ())),
+                preferred_element_type=jnp.float32)
+
+        each(first_tap, last_tap, one)
 
     def tile8(x):
         return pl.multiple_of(x, 8)
@@ -228,8 +244,8 @@
         high_at = -(-(half_rows + p * part_rows) // chan) if p else half_rows // chan
         low_end = min(-(-(p + 1) * part_rows // chan), half_rows // chan)
         high_end = -(-(half_rows + (p + 1) * part_rows) // chan)
-        weigh(list(range(low_at, low_end)))
-        weigh(list(range(high_at, high_end)))
+        weigh(low_at, low_end)
+        weigh(high_at, high_end)
         for s in range(2):
             src = tile8((1 - mine) * half_rows + p * part_rows + starts_of[s])
             flight[p, s] = send(wgrad.at[pl.ds(src, sizes_of[s])],
@@ -237,14 +253,14 @@
 
     reduce_stage(0, 0, [1])
     reduce_stage(0, 1, [1])
-    spread(range(3, 5))
+    spread(3, 5)
     reduce_stage(0, 0, [2])
     reduce_stage(0, 1, [2])
-    spread(range(5, 6))
+    spread(5, 6)
     reduce_stage(1, 0)
-    spread(range(6, 8))
+    spread(6, 8)
     reduce_stage(1, 1)
-    spread(range(8, 9))
+    spread(8, 9)
 
     entries = tgrad.shape[0] // VOXELS
     lane = lax.broadcasted_iota(jnp.int32, (1, 128), 1)
@@ -278,11 +294,14 @@
                  ("space", level)) for level in range(ls)]
 
     reduce_stage(2, 1)
-    third = TAPS // 3 * chan
-
-    def convolve(i):
-        return jnp.dot(cols[:, i * third:(i + 1) * third], ker[i * third:(i + 1) * third, :],
-                       preferred_element_type=jnp.float32)
+    conv[...] = patch[1:5, 1:5, 1:5].reshape(own, chan)
+
+    def convolve(first, last):
+        def one(row):
+            at = pl.ds(pl.multiple_of(row * 3 * chan, 3 * chan), 3 * chan)
+            conv[...] += jnp.dot(cols[:, at], ker[at, :], preferred_element_type=jnp.float32)
+
+        each(first, last, one)
 
     total = wsend[ld][0:1, :]
     kernel_scale = (ndp / total) * scale
@@ -327,11 +346,11 @@
         for p in range(3):
             to_other_core(p, s, offs[p, s], last)
 
-    conv[...] = convolve(0) + patch[1:5, 1:5, 1:5].reshape(own, chan)
+    convolve(0, 3)
     reduce_stage(3, 0)
-    conv[...] += convolve(1)
+    convolve(3, 6)
     reduce_stage(3, 1)
-    conv[...] += convolve(2)
+    convolve(6, 9)
     for v in range(VOXELS):
         gvox[pl.ds(v, bricks, stride=VOXELS), :] = conv[v * 8:(v + 1) * 8, :]
     out_f[0] = (gvox[...] * mask[...]).astype(jnp.bfloat16)
@@ -342,19 +361,21 @@
         copy.wait_recv()
     factor = own_weight * ndp / total
 
-    def feature_grads(some):
-        for b in some:
-            lo, hi = b * VOXELS, (b + 1) * VOXELS
-            held = gnat[lo:hi, :] + tgrad[lo:hi, :]
+    def feature_grads(first_brick, last_brick):
+        def one(b):
+            at = pl.ds(pl.multiple_of(b * VOXELS, VOXELS), VOXELS)
+            held = gnat[at, :] + tgrad[at, :]
             for e, chosen in enumerate(picks):
                 came = back_in[e * VOXELS:(e + 1) * VOXELS, :].astype(jnp.float32)
                 here = jnp.full((VOXELS, chan), chosen, jnp.int32) == b
                 held = held + jnp.where(here, came, 0.0)
-            out_g[0, lo:hi, :] = (factor * (mask[lo:hi, :] * held)).astype(jnp.bfloat16)
-
-    feature_grads(range(bricks // 2))
+            out_g[0, at, :] = (factor * (mask[at, :] * held)).astype(jnp.bfloat16)
+
+        each(first_brick, last_brick, one)
+
+    feature_grads(0, bricks // 2)
     finish(1)
-    feature_grads(range(bricks // 2, bricks))
+    feature_grads(bricks // 2, bricks)
     homes.append(pltpu.make_async_copy(out_g, home_g, load_sem.at[9]))
     homes[1].start()
     for j in (3, 2, 1):

time: 47.6 us -> 52.5 us (1.10)
  Pallas kernels: 46.1 us -> 51 us
    pallas_call x1, Pallas kernels: 43.7 us -> 48.6 us  [on_device(): pl.pallas_call(functools.partial(kernel_body, (nspace, ndp, cap, bricks,...]
where the time goes in v5:
time: 52.5 us; the launch traced here: 52.3 us
  Pallas kernels  51 us (97%)
  between operations  1.29 us (2%)
    pallas_call x1, Pallas kernels, on_device(): pl.pallas_call(functools.partial(kernel_body, (nspace, ndp, cap, bricks,...  48.6 us
    pallas_call x1, Pallas kernels, on_device(): pl.pallas_call(write_out, out_shape=tuple((jax.ShapeDtypeStruct(r.shape,...  2.45 us

profile of v5, /device:TPU:1, one launch (start us, length us, event | category | flops | bytes accessed | tf_op | source)
XLA Modules:
  0.0 52.3 jit_solution(14545369734474011315)
XLA Ops:
  1.3 48.6 %shard_map.94 = (bf16[1,512,128]{2,1,0:T(8,128)(2,1)}, bf16[1,512,128]{2,1,0:T(8,128)(2,1)}, f32[3456,128]{1,0:T(8,128)}) custom-call(bf16[1,512,128]{2,1,0:T(8,128)(2,1)} %feat_h.1, s32[1,512]{1,0:T(1,128)} %occ_h.1, s32[1,8,27]{2,1,0:T(8,128)} %pairs_h.1, s32[1,1,16]{2,1,0:T(1,128)} %sends_h.1, s32[1]{0:T(128)S(6)} %copy.10.weight_h, ...), custom_call_target="tpu_custom_call" | custom-call | flops 1358954496 | bytes 6291456 | tf_op jit(solution)/shard_map/pallas_call | solution.py:436
  49.9 2.5 %shard_map.95 = (bf16[1,512,128]{2,1,0:T(8,128)(2,1)}, bf16[1,512,128]{2,1,0:T(8,128)(2,1)}, f32[3456,128]{1,0:T(8,128)}) custom-call(bf16[1,512,128]{2,1,0:T(8,128)(2,1)} %get-tuple-element.6.in_f, bf16[1,512,128]{2,1,0:T(8,128)(2,1)} %get-tuple-element.7.in_g, f32[3456,128]{1,0:T(8,128)} %get-tuple-element.8.in_k), custom_call_target="tpu_custom_call" | custom-call | bytes 4194304 | tf_op jit(solution)/shard_map/pallas_call | solution.py:489

commit v6 on v4

--- a/solution.py
+++ b/solution.py
@@ -261,6 +261,7 @@
     for turn_of, (offsets, voxels) in enumerate(voxel_classes().items()):
         if turn_of == 14:
             reduce_stage(2, 0)
+            reduce_stage(2, 1)
         left = jnp.concatenate([hits[o] for o in offsets] * 2, axis=0).astype(jnp.bfloat16)
         right = jnp.concatenate(
             [jnp.concatenate([pgrad[pos[j][0], pos[j][1], pos[j][2]] for _, pos in voxels], axis=1)
@@ -277,7 +278,6 @@
     back = [send(back_out.at[pl.ds(level * rows, rows)], back_in.at[pl.ds(level * rows, rows)],
                  ("space", level)) for level in range(ls)]
 
-    reduce_stage(2, 1)
     third = TAPS // 3 * chan
 
     def convolve(i):
@@ -327,17 +327,22 @@
         for p in range(3):
             to_other_core(p, s, offs[p, s], last)
 
+    reduce_stage(3, 0)
+    reduce_stage(3, 1)
     conv[...] = convolve(0) + patch[1:5, 1:5, 1:5].reshape(own, chan)
-    reduce_stage(3, 0)
+    finish(0)
     conv[...] += convolve(1)
-    reduce_stage(3, 1)
+    finish(1)
+    gather_take(3, 0)
+    gather_take(3, 1)
     conv[...] += convolve(2)
+    gather_take(2, 0)
+    gather_take(2, 1)
     for v in range(VOXELS):
         gvox[pl.ds(v, bricks, stride=VOXELS), :] = conv[v * 8:(v + 1) * 8, :]
     out_f[0] = (gvox[...] * mask[...]).astype(jnp.bfloat16)
     homes = [pltpu.make_async_copy(out_f, home_f, load_sem.at[8])]
     homes[0].start()
-    finish(0)
     for copy in back:
         copy.wait_recv()
     factor = own_weight * ndp / total
@@ -352,14 +357,11 @@
                 held = held + jnp.where(here, came, 0.0)
             out_g[0, lo:hi, :] = (factor * (mask[lo:hi, :] * held)).astype(jnp.bfloat16)
 
-    feature_grads(range(bricks // 2))
-    finish(1)
-    feature_grads(range(bricks // 2, bricks))
+    feature_grads(range(bricks))
     homes.append(pltpu.make_async_copy(out_g, home_g, load_sem.at[9]))
     homes[1].start()
-    for j in (3, 2, 1):
-        for s in range(2):
-            gather_take(j, s)
+    gather_take(1, 0)
+    gather_take(1, 1)
 
     def go_home(off, size):
         at = pl.ds(tile8(off), size)

time: 47.6 us -> 48.8 us (1.025)
  Pallas kernels: 46.1 us -> 47.3 us
    pallas_call x1, Pallas kernels: 43.7 us -> 44.9 us  [on_device(): pl.pallas_call(functools.partial(kernel_body, (nspace, ndp, cap, bricks,...]
where the time goes in v6:
time: 48.8 us; the launch traced here: 48.6 us
  Pallas kernels  47.3 us (97%)
  between operations  1.29 us (3%)
    pallas_call x1, Pallas kernels, on_device(): pl.pallas_call(functools.partial(kernel_body, (nspace, ndp, cap, bricks,...  44.9 us
    pallas_call x1, Pallas kernels, on_device(): pl.pallas_call(write_out, out_shape=tuple((jax.ShapeDtypeStruct(r.shape,...  2.45 us

profile of v6, /device:TPU:1, one launch (start us, length us, event | category | flops | bytes accessed | tf_op | source)
XLA Modules:
  0.0 48.6 jit_solution(3864907158856965556)
XLA Ops:
  1.3 44.9 %shard_map.94 = (bf16[1,512,128]{2,1,0:T(8,128)(2,1)}, bf16[1,512,128]{2,1,0:T(8,128)(2,1)}, f32[3456,128]{1,0:T(8,128)}) custom-call(bf16[1,512,128]{2,1,0:T(8,128)(2,1)} %feat_h.1, s32[1,512]{1,0:T(1,128)} %occ_h.1, s32[1,8,27]{2,1,0:T(8,128)} %pairs_h.1, s32[1,1,16]{2,1,0:T(1,128)} %sends_h.1, s32[1]{0:T(128)S(6)} %copy.10.weight_h, ...), custom_call_target="tpu_custom_call" | custom-call | flops 1358954496 | bytes 6291456 | tf_op jit(solution)/shard_map/pallas_call | solution.py:417
  46.1 2.5 %shard_map.95 = (bf16[1,512,128]{2,1,0:T(8,128)(2,1)}, bf16[1,512,128]{2,1,0:T(8,128)(2,1)}, f32[3456,128]{1,0:T(8,128)}) custom-call(bf16[1,512,128]{2,1,0:T(8,128)(2,1)} %get-tuple-element.6.in_f, bf16[1,512,128]{2,1,0:T(8,128)(2,1)} %get-tuple-element.7.in_g, f32[3456,128]{1,0:T(8,128)} %get-tuple-element.8.in_k), custom_call_target="tpu_custom_call" | custom-call | bytes 4194304 | tf_op jit(solution)/shard_map/pallas_call | solution.py:470
